TPU v7x, 128 devices: a whole 4x4x4 slice. The times are simulated.
128 devices in a mesh: sx: 4 (over y), sy: 4 (over x), gz: 8 (over z, core).
Axes of the slice: x: 4, y: 4, z: 4, core: 2. Of those that a mesh axis runs over, the one named last changes fastest.
Arguments:
- observed: float32 [512, 64, 512], P('gz', 'sx', 'sy'), may hold values from 0.25 to 2
- zone_of_slice: int32 [512], P('gz'), may hold values from 0 to 7
- lateral_x: float32 [8, 7], replicated, may hold values from 0.05 to 1
- lateral_y: float32 [8, 7], replicated, may hold values from 0.05 to 1
- depth_psf: float32 [17], replicated, may hold values from 0.05 to 1
- stitch_width: int32 [4, 4, 2], replicated, may hold values from 1 to 8
Outputs:
- estimate: float32 [512, 64, 512], P('gz', 'sx', 'sy')
All inputs are finite; a program needn't handle non-finite values.
Results may differ from a plain program's by a relative error of at most 0.0001.
Values sent between devices are 32-bit elements; how exact they have to be, the bound alone decides.
A program may use at most 64 MiB of HBM per device.

v0:
```python
import itertools
import jax
import jax.numpy as jnp
from jax import lax
from jax.experimental import pallas as pl
from jax.experimental.pallas import tpu as pltpu
from jax.sharding import PartitionSpec as P

MESH = pl.DeviceIdType.MESH
F32 = jnp.float32
BF16 = jnp.bfloat16
NX, NY, NZ = 16, 128, 64
R = 3
HZ = 16
EZ = NZ + 2 * HZ
EX = NX + 2 * R
SX, SY, GZ = 4, 4, 8
DIRS = [d for d in itertools.product((-1, 0, 1), repeat=3) if d != (0, 0, 0)]
SDIRS = [d for d in DIRS if d[2] == 0]
KX, KY, KYM, KYF = 0, 7, 14, 21


def kernel(
    obs, zone, lat_x, lat_y, psf, stitch, out,
    est1, est2, spr1, spr2, pk, ye1, ye2, ys1, ys2, lest, rnorm, res,
    ktab, taps, tb, in_sem, out_sem, t_sem,
    es1, er1, es2, er2, ss1, sr1, ss2, sr2,
):
    sx, sy, gz = lax.axis_index("sx"), lax.axis_index("sy"), lax.axis_index("gz")
    lane = lax.broadcasted_iota(jnp.int32, (8, 128), 1)
    lane6 = lane % 6
    edge = jnp.logical_or(lane < R, lane >= NY - R)

    loads = [pltpu.make_async_copy(obs.at[:, x, :], est1.at[R + x, pl.ds(HZ, NZ)], in_sem.at[x]) for x in range(NX)]
    for c in loads:
        c.start()

    def inside(dx, dy):
        ok = None
        for at, d, n in ((sx, dx, SX), (sy, dy, SY)):
            if d:
                t = at < n - 1 if d > 0 else at > 0
                ok = t if ok is None else jnp.logical_and(ok, t)
        return ok

    def guarded(cond, fn):
        if cond is None:
            fn()
        else:
            pl.when(cond)(fn)

    def device(dx, dy, dz):
        return (sx + dx, sy + dy, lax.rem(gz + dz + GZ, GZ))

    for dx, slot, rows in ((1, 0, 0), (-1, 2, EX - R)):
        @pl.when(jnp.logical_not(inside(-dx, 0)))
        def _(slot=slot, rows=rows):
            for e in (est1, est2, spr1, spr2):
                e[pl.ds(rows, R)] = jnp.zeros((R,) + e.shape[1:], F32)
            for y in (ye1, ye2, ys1, ys2):
                for side in range(2):
                    y[side, slot] = jnp.zeros(y.shape[2:], F32)
    for dy, side in ((1, 0), (-1, 1)):
        @pl.when(jnp.logical_not(inside(0, -dy)))
        def _(side=side):
            for y in (ye1, ye2, ys1, ys2):
                y[side] = jnp.zeros(y.shape[1:], F32)

    barrier = pltpu.get_barrier_semaphore()
    for dx, dy in itertools.product((-1, 0, 1), repeat=2):
        def greet(dx=dx, dy=dy):
            for dz in (-1, 0, 1):
                if (dx, dy, dz) != (0, 0, 0):
                    pl.semaphore_signal(barrier, inc=1, device_id=device(dx, dy, dz), device_id_type=MESH)
        guarded(inside(dx, dy), greet)

    ktab[...] = jnp.zeros((8, 128), F32)
    ktab[:, 0:7] = lat_x[...]
    ktab[:, 7:14] = lat_y[...]
    for z in range(NZ):
        taps[HZ + z : HZ + z + 1, :] = ktab[pl.ds(zone[z], 1), :]

    def make_taps(g, _):
        rows = pl.ds(pl.multiple_of(g * 8, 8), 8)
        t = taps[rows, :]
        for i in range(14):
            tb[i, rows, :] = jnp.broadcast_to(t[:, i : i + 1], (8, 128))
        for b in range(7):
            reach = lane + (b - R)
            ok = jnp.logical_and(reach >= 0, reach < NY)
            tb[KYM + b, rows, :] = jnp.where(ok, tb[KY + b, rows, :], 0.0)
            tb[KYF + b, rows, :] = jnp.where(ok, tb[KY + 6 - b, rows, :], 0.0)
        return 0

    lax.fori_loop(2, 10, make_taps, 0)

    def pack(src, off, dst):
        def body(g, _):
            rows = pl.ds(pl.multiple_of(g * 8 + off, 8), 8)
            acc = jnp.zeros((8, 128), F32)
            for x in range(NX):
                v = pltpu.roll(src[R + x, rows, :], 6 * x + R, 1)
                acc = jnp.where(jnp.logical_and(lane >= 6 * x, lane < 6 * x + 6), v, acc)
            dst[pl.ds(pl.multiple_of(g * 8, 8), 8), :] = acc
            return 0

        lax.fori_loop(0, NZ // 8, body, 0)

    def copies(main, strips, packed, halo, dirs, send, recv):
        found = {}
        for i, (dx, dy, dz) in enumerate(dirs):
            zs, zd, n = {0: (0, halo, NZ), 1: (NZ - HZ, 0, HZ), -1: (0, halo + NZ, HZ)}[dz]
            if dy == 0:
                xs, xd, m = {0: (R, R, NX), 1: (NX, 0, R), -1: (R, R + NX, R)}[dx]
                src = main.at[pl.ds(xs, m), pl.ds(halo + zs, n), :]
                dst = main.at[pl.ds(xd, m), pl.ds(zd, n), :]
            else:
                src = packed.at[pl.ds(zs, n), :]
                dst = strips.at[0 if dy > 0 else 1, 1 - dx, pl.ds(zd, n), :]
            found[(dx, dy, dz)] = pltpu.make_async_remote_copy(
                src_ref=src, dst_ref=dst, send_sem=send.at[i], recv_sem=recv.at[i],
                device_id=device(dx, dy, dz), device_id_type=MESH)
        return found

    def each(found, sign, what):
        for dx, dy in sorted({d[:2] for d in found}, key=lambda d: -abs(d[0]) - abs(d[1])):
            def go(dx=dx, dy=dy):
                for d, c in found.items():
                    if d[:2] == (dx, dy):
                        getattr(c, what)()
            guarded(inside(sign * dx, sign * dy), go)

    def lateral(rows_of, strips_of, flip, sink, lo, hi, off):
        def body(g, _):
            trow = pl.ds(pl.multiple_of(g * 8 + off, 8), 8)
            kx = [tb[KX + (6 - a if flip else a), trow, :] for a in range(7)]
            ky = [tb[KY + (6 - b if flip else b), trow, :] for b in range(7)]
            c, cu, cd = strips_of(g)
            cu, cd = pltpu.roll(cu, 32, 1), pltpu.roll(cd, 96, 1)
            c2 = jnp.where(lane < 96, c, cd)
            c1 = jnp.where(lane < 110, c2, cu)
            al = kx[3] * c
            for a in (0, 1, 2, 4, 5, 6):
                al = al + kx[a] * pltpu.roll(c2 if a == 6 else c1, (18 - 6 * a) % 128, 1)
            sc = jnp.zeros((8, 128), F32)
            for b in (0, 1, 2, 4, 5, 6):
                ok = {0: lane6 >= 3, 1: jnp.logical_or(lane6 == 3, lane6 == 4), 2: lane6 == 3,
                      4: lane6 == 2, 5: jnp.logical_or(lane6 == 1, lane6 == 2), 6: lane6 <= 2}[b]
                sc = sc + jnp.where(ok, ky[b] * pltpu.roll(al, (R - b) % 128, 1), 0.0)
            kym = [tb[(KYF if flip else KYM) + b, trow, :] for b in range(7)]
            window = [rows_of(x, g) for x in range(6)]
            for x in range(NX):
                window.append(rows_of(x + 6, g))
                along = kx[0] * window[0]
                for a in range(1, 7):
                    along = along + kx[a] * window[a]
                window = window[1:]
                acc = kym[3] * along
                for b in (0, 1, 2, 4, 5, 6):
                    acc = acc + kym[b] * pltpu.roll(along, (R - b) % 128, 1)
                acc = acc + jnp.where(edge, pltpu.roll(sc, (-(6 * x + R)) % 128, 1), 0.0)
                sink(x, g, acc)
            return 0

        lax.fori_loop(lo, hi, body, 0)

    def rows_from(ref):
        return lambda x, g: ref[x, pl.ds(pl.multiple_of(g * 8, 8), 8), :]

    left = lane6 < R

    def strips_from(ref):
        def get(g):
            r = pl.ds(pl.multiple_of(g * 8, 8), 8)
            return tuple(jnp.where(left, ref[0, s, r, :], ref[1, s, r, :]) for s in (1, 0, 2))
        return get

    def band(i, j, k):
        return stitch[jnp.clip(sx + i, 0, SX - 1), jnp.clip(sy + j, 0, SY - 1), k]

    def half(pos, width):
        return jnp.where(pos < width, 0.5, 1.0).astype(F32)

    wrows = []
    for x in range(-R, NX + R):
        i = -1 if x < 0 else (1 if x >= NX else 0)
        row = half(jnp.full((8, 128), x - i * NX, jnp.int32), band(i, 0, 0)) * half(lane, band(i, 0, 1))
        cond = inside(i, 0)
        if cond is not None:
            row = row * jnp.where(cond, 1.0, 0.0).astype(F32)
        wrows.append(row)
    wstrips = []
    for i in (0, -1, 1):
        parts = []
        for j, pos in ((-1, NY - R + lane6), (1, lane6 - R)):
            v = half(lane // 6, band(i, j, 0)) * half(pos, band(i, j, 1))
            parts.append(v * jnp.where(inside(i, j), 1.0, 0.0).astype(F32))
        wstrips.append(jnp.where(left, parts[0], parts[1]))

    total = psf[0]
    for j in range(1, 17):
        total = total + psf[j]

    def depth_matrix(m, k, forward):
        off = lax.broadcasted_iota(jnp.int32, (m, k), 1) - lax.broadcasted_iota(jnp.int32, (m, k), 0)
        h = jnp.zeros((m, k), F32)
        for j in range(17):
            h = jnp.where(off == j, psf[16 - j if forward else j], h)
        h = h / jnp.full((m, k), total, F32)
        hi = h.astype(BF16)
        lo = (h - hi.astype(F32)).astype(BF16)
        return jnp.concatenate([hi, hi, lo], axis=1)

    def split3(v):
        hi = v.astype(BF16)
        lo = (v - hi.astype(F32)).astype(BF16)
        return hi, lo

    for c in loads:
        c.wait()
    pack(est1, HZ, pk.at[0])
    nx = 3 - (sx == 0).astype(jnp.int32) - (sx == SX - 1).astype(jnp.int32)
    ny = 3 - (sy == 0).astype(jnp.int32) - (sy == SY - 1).astype(jnp.int32)
    pl.semaphore_wait(barrier, nx * ny * 3 - 1)

    tcopies = [
        pltpu.make_async_remote_copy(
            src_ref=taps.at[pl.ds(s, HZ), :], dst_ref=taps.at[pl.ds(d, HZ), :],
            send_sem=t_sem.at[0, i], recv_sem=t_sem.at[1, i], device_id=device(0, 0, dz), device_id_type=MESH)
        for i, (dz, s, d) in enumerate(((1, NZ, 0), (-1, HZ, HZ + NZ)))
    ]
    for c in tcopies:
        c.start()
    e1 = copies(est1, ye1, pk.at[0], HZ, DIRS, es1, er1)
    s1 = copies(spr1, ys1, pk.at[1], 0, SDIRS, ss1, sr1)
    e2 = copies(est2, ye2, pk.at[2], HZ, DIRS, es2, er2)
    s2 = copies(spr2, ys2, pk.at[3], 0, SDIRS, ss2, sr2)
    each(e1, 1, "start")

    def keep_norm(x, g, v):
        rnorm[x, pl.ds(pl.multiple_of(g * 8, 8), 8), :] = 1.0 / v

    lateral(lambda x, g: wrows[x], lambda g: wstrips, True, keep_norm, 0, NZ // 8, HZ)
    for c in tcopies:
        c.wait_recv()
    lax.fori_loop(0, 2, make_taps, 0)
    lax.fori_loop(10, 12, make_taps, 0)

    fwd1 = depth_matrix(48, 64, True)
    fwd2 = depth_matrix(32, 48, True)
    bwd = depth_matrix(64, 80, False)

    def keep_lest(x, g, v):
        lest[x, pl.ds(pl.multiple_of(g * 8, 8), 8), :] = v

    for est, ye, ecop, spr, ys, scop, pks, last in (
        (est1, ye1, e1, spr1, ys1, s1, 1, False),
        (est2, ye2, e2, spr2, ys2, s2, 3, True),
    ):
        each(ecop, -1, "wait_recv")
        lateral(rows_from(est), strips_from(ye), False, keep_lest, 0, EZ // 8, 0)
        for p in (0, 1, 6, 7, 2, 3, 4, 5):
            a, b = 2 * p, 2 * p + 1
            hi, lo = split3(jnp.concatenate([lest[a], lest[b]], axis=1))
            top = jnp.concatenate([hi[0:64], lo[0:64], hi[0:64]], axis=0)
            low = jnp.concatenate([hi[48:96], lo[48:96], hi[48:96]], axis=0)
            blur = jnp.concatenate(
                [jnp.dot(fwd1, top, preferred_element_type=F32), jnp.dot(fwd2, low, preferred_element_type=F32)], axis=0)
            wide = jnp.concatenate([wrows[R + a][0:1], wrows[R + b][0:1]], axis=1)
            seen = jnp.concatenate([est1[R + a, 8:88, :], est1[R + b, 8:88, :]], axis=1)
            hi, lo = split3(wide * seen / blur)
            back = jnp.dot(bwd, jnp.concatenate([hi, lo, hi], axis=0), preferred_element_type=F32)
            spr[R + a] = back[:, 0:128]
            spr[R + b] = back[:, 128:256]
        pack(spr, 0, pk.at[pks])
        each(scop, 1, "start")
        each(scop, -1, "wait_recv")

        def keep_est(x, g, v, est=est, last=last):
            r = pl.ds(pl.multiple_of(g * 8, 8), 8)
            rz = pl.ds(pl.multiple_of(g * 8 + HZ, 8), 8)
            new = est[R + x, rz, :] * v * rnorm[x, r, :]
            if last:
                res[x, r, :] = new
            else:
                est2[R + x, rz, :] = new

        lateral(rows_from(spr), strips_from(ys), True, keep_est, 0, NZ // 8, HZ)
        if not last:
            pack(est2, HZ, pk.at[2])
            each(e2, 1, "start")

    stores = [pltpu.make_async_copy(res.at[x], out.at[:, x, :], out_sem.at[x]) for x in range(NX)]
    for c in stores:
        c.start()
    for c in tcopies:
        c.wait_send()
    for found in (e1, s1, e2, s2):
        each(found, 1, "wait_send")
    for c in stores:
        c.wait()


def body(observed, zone_of_slice, lateral_x, lateral_y, depth_psf, stitch_width):
    any_spec = pl.BlockSpec(memory_space=pl.ANY)
    smem = pl.BlockSpec(memory_space=pltpu.SMEM)
    vmem = pl.BlockSpec(memory_space=pltpu.VMEM)
    dma = pltpu.SemaphoreType.DMA
    ne, ns = len(DIRS), len(SDIRS)
    return pl.pallas_call(
        kernel,
        out_shape=jax.ShapeDtypeStruct(observed.shape, F32),
        in_specs=[any_spec, smem, vmem, vmem, smem, smem],
        out_specs=any_spec,
        scratch_shapes=[
            pltpu.VMEM((EX, EZ, NY), F32), pltpu.VMEM((EX, EZ, NY), F32),
            pltpu.VMEM((EX, NZ, NY), F32), pltpu.VMEM((EX, NZ, NY), F32),
            pltpu.VMEM((4, NZ, 128), F32),
            pltpu.VMEM((2, 3, EZ, 128), F32), pltpu.VMEM((2, 3, EZ, 128), F32),
            pltpu.VMEM((2, 3, NZ, 128), F32), pltpu.VMEM((2, 3, NZ, 128), F32),
            pltpu.VMEM((NX, EZ, NY), F32), pltpu.VMEM((NX, NZ, NY), F32), pltpu.VMEM((NX, NZ, NY), F32),
            pltpu.VMEM((8, 128), F32), pltpu.VMEM((EZ, 128), F32), pltpu.VMEM((28, EZ, 128), F32),
            dma((NX,)), dma((NX,)), dma((2, 2)),
            dma((ne,)), dma((ne,)), dma((ne,)), dma((ne,)),
            dma((ns,)), dma((ns,)), dma((ns,)), dma((ns,)),
        ],
        compiler_params=pltpu.CompilerParams(collective_id=0, has_side_effects=True, vmem_limit_bytes=40 * 1024 * 1024),
        name="deconvolve",
    )(observed, zone_of_slice, lateral_x, lateral_y, depth_psf, stitch_width)


def solution(mesh):
    in_specs = (P("gz", "sx", "sy"), P("gz"), P(), P(), P(), P())
    out_specs = P("gz", "sx", "sy")
    return jax.shard_map(body, mesh=mesh, in_specs=in_specs, out_specs=out_specs, check_vma=False)
```

profile of v0, /device:TPU:2, one launch (start us, length us, event | category | flops | bytes accessed | tf_op | source)
XLA Modules:
  0.0 52.6 jit_solution(14107213938852210388)
XLA Ops:
  0.0 0.0 copy-start.4
  0.0 0.0 copy-start.2
  0.0 0.0 copy-start.1
  0.0 0.0 copy-start.3
  0.0 0.8 %copy.7.stitch = s32[4,4,2]{2,1,0:T(4,128)S(1)} copy(s32[4,4,2]{1,2,0:T(2,128)} %param.11) | data formatting | bytes 256 | tf_op args[5]
  0.9 0.0 copy-done.4
  0.9 0.0 copy-done.2
  0.9 0.0 copy-done.1
  0.9 0.0 copy-done.3
  0.9 0.0 copy-start
  0.9 1.0 %copy-done = f32[64,16,128]{2,1,0:T(8,128)S(1)} copy-done((f32[64,16,128]{2,1,0:T(8,128)S(1)}, f32[64,16,128]{2,1,0:T(8,128)}, u32[]{:S(2)}) %copy-start) | copy-done | bytes 524312
  1.9 49.9 %deconvolve.1 = f32[64,16,128]{2,1,0:T(8,128)S(1)} custom-call(f32[64,16,128]{2,1,0:T(8,128)S(1)} %copy-done, s32[64]{0:T(128)S(1)} %copy-done.3, f32[8,7]{1,0:T(8,128)S(1)} %copy-done.1, f32[8,7]{1,0:T(8,128)S(1)} %copy-done.2, f32[17]{0:T(128)S(1)} %copy-done.4, s32[4,4,2]{2,1,0:T(4,128)S(1)} %copy.7.stitch), custom_call_target="tpu_custom_call" | custom-call | tf_op jit(solution)/shard_map/deconvolve/pallas_call | solution.py:310
  51.8 0.8 %copy.9 = f32[64,16,128]{2,1,0:T(8,128)} copy(f32[64,16,128]{2,1,0:T(8,128)S(1)} %deconvolve.1) | data formatting | bytes 1048576
Async XLA Ops:
  0.0 0.9 %copy-start.4 = (f32[17]{0:T(128)S(1)}, f32[17]{0:T(128)}, u32[]{:S(2)}) copy-start(f32[17]{0:T(128)} %psf.1) | copy-start | bytes 208
  0.0 0.9 %copy-start.2 = (f32[8,7]{1,0:T(8,128)S(1)}, f32[8,7]{1,0:T(8,128)}, u32[]{:S(2)}) copy-start(f32[8,7]{1,0:T(8,128)} %lat_y.1) | copy-start | bytes 676
  0.0 0.9 %copy-start.1 = (f32[8,7]{1,0:T(8,128)S(1)}, f32[8,7]{1,0:T(8,128)}, u32[]{:S(2)}) copy-start(f32[8,7]{1,0:T(8,128)} %lat_x.1) | copy-start | bytes 676
  0.0 0.9 %copy-start.3 = (s32[64]{0:T(128)S(1)}, s32[64]{0:T(128)}, u32[]{:S(2)}) copy-start(s32[64]{0:T(128)} %zone.1) | copy-start | bytes 772
  0.9 1.0 %copy-start = (f32[64,16,128]{2,1,0:T(8,128)S(1)}, f32[64,16,128]{2,1,0:T(8,128)}, u32[]{:S(2)}) copy-start(f32[64,16,128]{2,1,0:T(8,128)} %obs.1) | copy-start | bytes 1572868
where the time goes:
time: 52.8 us; the launch traced here: 52.6 us
  Pallas kernels  49.9 us (95%)
  local copies, waits for them, and re-layouts  2.68 us (5%)
    pallas_call x1, Pallas kernels, body(): pl.pallas_call(kernel, out_shape=jax.ShapeDtypeStruct(observed.shape, F32...  49.9 us
    unnamed x12, local copies, waits for them, and re-layouts  2.68 us

commit v1 on v0

v1 whole, which is shorter than its diff:
```python
import itertools
import jax
import jax.numpy as jnp
from jax import lax
from jax.experimental import pallas as pl
from jax.experimental.pallas import tpu as pltpu
from jax.sharding import PartitionSpec as P

MESH = pl.DeviceIdType.MESH
F32 = jnp.float32
BF16 = jnp.bfloat16
NX, NY, NZ = 16, 128, 64
R = 3
HZ = 16
EZ = NZ + 2 * HZ
EX = NX + 2 * R
SX, SY, GZ = 4, 4, 8
DIRS = [d for d in itertools.product((-1, 0, 1), repeat=3) if d != (0, 0, 0)]
SDIRS = [d for d in DIRS if d[2] == 0]
KX, KY = 0, 7
PAIRS = ((0, 1), (2, 4), (5, 6))
CORNERS = {(1, 1): (78, 110), (1, -1): (81, 113), (-1, 1): (0, 96), (-1, -1): (3, 99)}


def kernel(
    obs, zone, lat_x, lat_y, psf, stitch, out,
    est1, est2, spr1, spr2, pk, qk, ye1, ye2, ys1, ys2, qe1, qe2, qs1, qs2, ch, lest, rnorm, res,
    ktab, taps, tb, smat, in_sem, out_sem, t_sem,
    es1, er1, es2, er2, ss1, sr1, ss2, sr2,
):
    sx, sy, gz = lax.axis_index("sx"), lax.axis_index("sy"), lax.axis_index("gz")
    lane = lax.broadcasted_iota(jnp.int32, (8, 128), 1)
    lane6 = lane % 6
    edge = jnp.logical_or(lane < R, lane >= NY - R)

    loads = [pltpu.make_async_copy(obs.at[:, x, :], est1.at[R + x, pl.ds(HZ, NZ)], in_sem.at[x]) for x in range(NX)]
    for c in loads:
        c.start()

    def inside(dx, dy):
        ok = None
        for at, d, n in ((sx, dx, SX), (sy, dy, SY)):
            if d:
                t = at < n - 1 if d > 0 else at > 0
                ok = t if ok is None else jnp.logical_and(ok, t)
        return ok

    def guarded(cond, fn):
        if cond is None:
            fn()
        else:
            pl.when(cond)(fn)

    def device(dx, dy, dz):
        return (sx + dx, sy + dy, lax.rem(gz + dz + GZ, GZ))

    for dx, slot, rows in ((1, 0, 0), (-1, 1, EX - R)):
        @pl.when(jnp.logical_not(inside(-dx, 0)))
        def _(slot=slot, rows=rows):
            for e in (est1, est2, spr1, spr2):
                e[pl.ds(rows, R)] = jnp.zeros((R,) + e.shape[1:], F32)
            for q in (qe1, qe2, qs1, qs2):
                for side in range(2):
                    q[side, slot] = jnp.zeros(q.shape[2:], F32)
    for dy, side in ((1, 0), (-1, 1)):
        @pl.when(jnp.logical_not(inside(0, -dy)))
        def _(side=side):
            for y in (ye1, ye2, ys1, ys2, qe1, qe2, qs1, qs2):
                y[side] = jnp.zeros(y.shape[1:], F32)

    barrier = pltpu.get_barrier_semaphore()
    for dx, dy in itertools.product((-1, 0, 1), repeat=2):
        def greet(dx=dx, dy=dy):
            for dz in (-1, 0, 1):
                if (dx, dy, dz) != (0, 0, 0):
                    pl.semaphore_signal(barrier, inc=1, device_id=device(dx, dy, dz), device_id_type=MESH)
        guarded(inside(dx, dy), greet)

    ktab[...] = jnp.zeros((8, 128), F32)
    ktab[:, 0:7] = lat_x[...]
    ktab[:, 7:14] = lat_y[...]
    for z in range(NZ):
        taps[HZ + z : HZ + z + 1, :] = ktab[pl.ds(zone[z], 1), :]

    def make_taps(g, _):
        rows = pl.ds(pl.multiple_of(g * 8, 8), 8)
        t = taps[rows, :]
        for i in range(14):
            tb[i, rows, :] = jnp.broadcast_to(t[:, i : i + 1], (8, 128))
        return 0


    def place(acc, v, x):
        at = jnp.logical_and(lane >= 6 * x, lane < 6 * x + 6)
        return jnp.where(at, pltpu.roll(v, 6 * x + R, 1), acc)

    def pack_loop(src, off, dst):
        def body(g, _):
            acc = jnp.zeros((8, 128), F32)
            for x in range(NX):
                acc = place(acc, src[R + x, pl.ds(pl.multiple_of(g * 8 + off, 8), 8), :], x)
            dst[pl.ds(pl.multiple_of(g * 8, 8), 8), :] = acc
            return 0

        lax.fori_loop(0, NZ // 8, body, 0)

    def pack_corners(groups, dst):
        for k, (first, _) in enumerate(CORNERS.values()):
            acc = jnp.zeros((8, 128), F32)
            for g in range(NZ // 8):
                at = jnp.logical_and(lane >= 16 * g, lane < 16 * g + 16)
                acc = jnp.where(at, pltpu.roll(groups[g], (16 * g - first) % 128, 1), acc)
            dst[k] = acc

    def unpack_corners(src, halo):
        up = (lane + 4) % 6 < R
        for g in range((NZ + 2 * halo) // 8):
            slot, local = 1, g - halo // 8
            if local < 0:
                slot, local = 0, local + NZ // 8
            elif local >= NZ // 8:
                slot, local = 2, local - NZ // 8
            got = [pltpu.roll(src[0 if d[1] > 0 else 1, 0 if d[0] > 0 else 1, slot], (at - 16 * local) % 128, 1)
                   for d, (_, at) in CORNERS.items()]
            cu = jnp.where(up, got[0], got[1])
            cd = jnp.where(left, got[2], got[3])
            ch[0, g * 8 : g * 8 + 8, :] = jnp.where(lane < 110, cd, cu)
            ch[1, g * 8 : g * 8 + 8, :] = cd

    def copies(main, strips, packed, corners, cpacked, halo, dirs, send, recv):
        found = {}
        for i, (dx, dy, dz) in enumerate(dirs):
            zs, zd, n = {0: (0, halo, NZ), 1: (NZ - HZ, 0, HZ), -1: (0, halo + NZ, HZ)}[dz]
            if dy == 0:
                xs, xd, m = {0: (R, R, NX), 1: (NX, 0, R), -1: (R, R + NX, R)}[dx]
                src = main.at[pl.ds(xs, m), pl.ds(halo + zs, n), :]
                dst = main.at[pl.ds(xd, m), pl.ds(zd, n), :]
            elif dx == 0:
                src = packed.at[pl.ds(zs, n), :]
                dst = strips.at[0 if dy > 0 else 1, pl.ds(zd, n), :]
            else:
                src = cpacked.at[list(CORNERS).index((dx, dy))]
                dst = corners.at[0 if dy > 0 else 1, 0 if dx > 0 else 1, 1 - dz]
            found[(dx, dy, dz)] = pltpu.make_async_remote_copy(
                src_ref=src, dst_ref=dst, send_sem=send.at[i], recv_sem=recv.at[i],
                device_id=device(dx, dy, dz), device_id_type=MESH)
        return found

    ALL = ((1, 0), (-1, 0), (0, 0), (1, 1), (1, -1), (-1, 1), (-1, -1), (0, 1), (0, -1))
    MAIN, CORN, SIDE = ALL[:3], ALL[3:7], ALL[7:]

    def each(found, sign, what, order=ALL):
        for dx, dy in order:
            if not any(d[:2] == (dx, dy) for d in found):
                continue

            def go(dx=dx, dy=dy):
                for dz in (0, 1, -1):
                    if (dx, dy, dz) in found:
                        getattr(found[(dx, dy, dz)], what)()
            guarded(inside(sign * dx, sign * dy), go)

    def lateral(rows_of, strips_of, flip, sink, lo, hi, off):
        def body(g, _):
            trow = pl.ds(pl.multiple_of(g * 8 + off, 8), 8)
            kx = [tb[KX + (6 - a if flip else a), trow, :] for a in range(7)]
            ky = [tb[KY + (6 - b if flip else b), trow, :] for b in range(7)]
            c, c1, c2 = strips_of(g)
            c1, c2 = jnp.where(lane < 96, c, c1), jnp.where(lane < 96, c, c2)
            al = kx[3] * c
            for a in (0, 1, 2, 4, 5, 6):
                al = al + kx[a] * pltpu.roll(c2 if a == 6 else c1, (18 - 6 * a) % 128, 1)
            sc = jnp.zeros((8, 128), F32)
            for b in (0, 1, 2, 4, 5, 6):
                ok = {0: lane6 >= 3, 1: jnp.logical_or(lane6 == 3, lane6 == 4), 2: lane6 == 3,
                      4: lane6 == 2, 5: jnp.logical_or(lane6 == 1, lane6 == 2), 6: lane6 <= 2}[b]
                sc = sc + jnp.where(ok, ky[b] * pltpu.roll(al, (R - b) % 128, 1), 0.0)
            window = [rows_of(x, g) for x in range(6)]
            along = []
            for x in range(NX):
                window.append(rows_of(x + 6, g))
                v = kx[0] * window[x]
                for a in range(1, 7):
                    v = v + kx[a] * window[x + a]
                along.append(v)
            hi, lo = split3(jnp.concatenate(along, axis=0))
            both = jnp.concatenate([hi, lo], axis=1)
            acc = [ky[R] * v for v in along]
            for n, (b0, b1) in enumerate(PAIRS):
                moved = jnp.dot(both, smat[n], preferred_element_type=F32)
                for x in range(NX):
                    acc[x] = acc[x] + ky[b0] * moved[8 * x : 8 * x + 8, 0:128] + ky[b1] * moved[8 * x : 8 * x + 8, 128:256]
            done = []
            for x in range(NX):
                done.append(acc[x] + jnp.where(edge, pltpu.roll(sc, (-(6 * x + R)) % 128, 1), 0.0))
            sink(g, done)
            return 0

        lax.fori_loop(lo, hi, body, 0)

    def rows_from(ref):
        return lambda x, g: ref[x, pl.ds(pl.multiple_of(g * 8, 8), 8), :]

    left = lane6 < R

    def strips_from(ref):
        def get(g):
            r = pl.ds(pl.multiple_of(g * 8, 8), 8)
            return jnp.where(left, ref[0, r, :], ref[1, r, :]), ch[0, r, :], ch[1, r, :]
        return get

    def band(i, j, k):
        row = stitch[pl.ds(jnp.clip(sx + i, 0, SX - 1), 1), pl.ds(jnp.clip(sy + j, 0, SY - 1), 1), :]
        return jnp.broadcast_to(row[0, :, k : k + 1], (8, 128))

    def half(pos, width):
        return jnp.where(pos < width, 0.5, 1.0).astype(F32)

    bands = {(i, j): (band(i, j, 0), band(i, j, 1)) for i in (-1, 0, 1) for j in (-1, 0, 1)}
    wrows = []
    for x in range(-R, NX + R):
        i = -1 if x < 0 else (1 if x >= NX else 0)
        row = half(jnp.full((8, 128), x - i * NX, jnp.int32), bands[i, 0][0]) * half(lane, bands[i, 0][1])
        cond = inside(i, 0)
        if cond is not None:
            row = row * jnp.where(cond, 1.0, 0.0).astype(F32)
        wrows.append(row)
    wpos = {0: lane // 6, -1: NX - R + (lane - 110) // 6, 1: (lane - 96) // 6}
    wstrips = []
    for i in (0, -1, 1):
        lane_i = (lane + 4) % 6 if i < 0 else lane6
        parts = []
        for j, pos in ((-1, NY - R + lane_i), (1, lane_i - R)):
            v = half(wpos[i], bands[i, j][0]) * half(pos, bands[i, j][1])
            parts.append(v * jnp.where(inside(i, j), 1.0, 0.0).astype(F32))
        wstrips.append(jnp.where(lane_i < R, parts[0], parts[1]))
    wstrips_at = (wstrips[0], jnp.where(lane < 110, wstrips[2], wstrips[1]), wstrips[2])

    total = psf[0]
    for j in range(1, 17):
        total = total + psf[j]

    def depth_matrix(m, k, forward):
        off = lax.broadcasted_iota(jnp.int32, (m, k), 1) - lax.broadcasted_iota(jnp.int32, (m, k), 0)
        h = jnp.zeros((m, k), F32)
        for j in range(17):
            h = jnp.where(off == j, psf[16 - j if forward else j], h)
        h = h / jnp.full((m, k), total, F32)
        hi = h.astype(BF16)
        lo = (h - hi.astype(F32)).astype(BF16)
        return jnp.concatenate([hi, hi, lo], axis=1)

    def split3(v):
        hi = v.astype(BF16)
        lo = (v - hi.astype(F32)).astype(BF16)
        return hi, lo

    nx = 3 - (sx == 0).astype(jnp.int32) - (sx == SX - 1).astype(jnp.int32)
    ny = 3 - (sy == 0).astype(jnp.int32) - (sy == SY - 1).astype(jnp.int32)
    for c in loads:
        c.wait()
    pl.semaphore_wait(barrier, nx * ny * 3 - 1)

    tcopies = [
        pltpu.make_async_remote_copy(
            src_ref=taps.at[pl.ds(s, HZ), :], dst_ref=taps.at[pl.ds(d, HZ), :],
            send_sem=t_sem.at[0, i], recv_sem=t_sem.at[1, i], device_id=device(0, 0, dz), device_id_type=MESH)
        for i, (dz, s, d) in enumerate(((1, NZ, 0), (-1, HZ, HZ + NZ)))
    ]
    for c in tcopies:
        c.start()
    e1 = copies(est1, ye1, pk.at[0], qe1, qk.at[0], HZ, DIRS, es1, er1)
    s1 = copies(spr1, ys1, pk.at[1], qs1, qk.at[1], 0, SDIRS, ss1, sr1)
    e2 = copies(est2, ye2, pk.at[2], qe2, qk.at[2], HZ, DIRS, es2, er2)
    s2 = copies(spr2, ys2, pk.at[3], qs2, qk.at[3], 0, SDIRS, ss2, sr2)

    def packed_groups(k):
        return [pk[k, 8 * g : 8 * g + 8, :] for g in range(NZ // 8)]

    each(e1, 1, "start", MAIN)
    pack_loop(est1, HZ, pk.at[0])
    pack_corners(packed_groups(0), qk.at[0])
    each(e1, 1, "start", CORN + SIDE)

    row = lax.broadcasted_iota(jnp.int32, (256, 128), 0) % 128
    col = lax.broadcasted_iota(jnp.int32, (256, 128), 1)
    for n, pair in enumerate(PAIRS):
        for k, b in enumerate(pair):
            smat[n, :, 128 * k : 128 * k + 128] = jnp.where(row == col + (b - R), 1.0, 0.0).astype(BF16)
    lax.fori_loop(2, 10, make_taps, 0)

    def reciprocal(v):
        r = pltpu.reciprocal(v, approx=True)
        return r * (2.0 - v * r)

    def keep_norm(g, values):
        for x, v in enumerate(values):
            rnorm[x, pl.ds(pl.multiple_of(g * 8, 8), 8), :] = reciprocal(v)

    lateral(lambda x, g: wrows[x], lambda g: wstrips_at, True, keep_norm, 0, NZ // 8, HZ)
    fwd1 = depth_matrix(48, 64, True)
    fwd2 = depth_matrix(32, 48, True)
    bwd = depth_matrix(64, 80, False)
    for c in tcopies:
        c.wait_recv()
    lax.fori_loop(0, 2, make_taps, 0)
    lax.fori_loop(10, 12, make_taps, 0)

    def keep_lest(g, values):
        for x, v in enumerate(values):
            lest[x, pl.ds(pl.multiple_of(g * 8, 8), 8), :] = v

    for est, ye, qe, ecop, spr, ys, qs, scop, pks, last in (
        (est1, ye1, qe1, e1, spr1, ys1, qs1, s1, 1, False),
        (est2, ye2, qe2, e2, spr2, ys2, qs2, s2, 3, True),
    ):
        each(ecop, -1, "wait_recv")
        unpack_corners(qe, HZ)
        lateral(rows_from(est), strips_from(ye), False, keep_lest, 0, EZ // 8, 0)
        strip = [jnp.zeros((8, 128), F32) for _ in range(NZ // 8)]
        for part in ((0, 1, 6, 7), (2, 3, 4, 5)):
            blurs = []
            for p in part:
                hi, lo = split3(jnp.concatenate([lest[2 * p], lest[2 * p + 1]], axis=1))
                top = jnp.concatenate([hi[0:64], lo[0:64], hi[0:64]], axis=0)
                low = jnp.concatenate([hi[48:96], lo[48:96], hi[48:96]], axis=0)
                blurs.append(jnp.concatenate(
                    [jnp.dot(fwd1, top, preferred_element_type=F32), jnp.dot(fwd2, low, preferred_element_type=F32)], axis=0))
            for p, blur in zip(part, blurs):
                a, b = 2 * p, 2 * p + 1
                wide = jnp.concatenate([wrows[R + a][0:1], wrows[R + b][0:1]], axis=1)
                seen = jnp.concatenate([est1[R + a, 8:88, :], est1[R + b, 8:88, :]], axis=1)
                hi, lo = split3(wide * seen * reciprocal(blur))
                back = jnp.dot(bwd, jnp.concatenate([hi, lo, hi], axis=0), preferred_element_type=F32)
                for x, v in ((a, back[:, 0:128]), (b, back[:, 128:256])):
                    spr[R + x] = v
                    strip = [place(t, v[8 * g : 8 * g + 8], x) for g, t in enumerate(strip)]
            if part[0] == 0:
                pack_corners(strip, qk.at[pks])
                each(scop, 1, "start", MAIN + CORN)
            else:
                for g, t in enumerate(strip):
                    pk[pks, 8 * g : 8 * g + 8, :] = t
        each(scop, 1, "start", SIDE)
        each(scop, -1, "wait_recv")
        unpack_corners(qs, 0)

        def keep_est(g, values, est=est, last=last):
            r = pl.ds(pl.multiple_of(g * 8, 8), 8)
            rz = pl.ds(pl.multiple_of(g * 8 + HZ, 8), 8)
            acc = jnp.zeros((8, 128), F32)
            for x, v in enumerate(values):
                new = est[R + x, rz, :] * v * rnorm[x, r, :]
                if last:
                    res[x, r, :] = new
                else:
                    est2[R + x, rz, :] = new
                    acc = place(acc, new, x)
            if not last:
                pk[2, r, :] = acc

        lateral(rows_from(spr), strips_from(ys), True, keep_est, 0, NZ // 8, HZ)
        if not last:
            each(e2, 1, "start", MAIN)
            pack_corners(packed_groups(2), qk.at[2])
            each(e2, 1, "start", CORN + SIDE)

    stores = [pltpu.make_async_copy(res.at[x], out.at[:, x, :], out_sem.at[x]) for x in range(NX)]
    for c in stores:
        c.start()
    for c in tcopies:
        c.wait_send()
    for found in (e1, s1, e2, s2):
        each(found, 1, "wait_send")
    for c in stores:
        c.wait()


def body(observed, zone_of_slice, lateral_x, lateral_y, depth_psf, stitch_width):
    hbm = pl.BlockSpec(memory_space=pltpu.HBM)
    smem = pl.BlockSpec(memory_space=pltpu.SMEM)
    vmem = pl.BlockSpec(memory_space=pltpu.VMEM)
    dma = pltpu.SemaphoreType.DMA
    ne, ns = len(DIRS), len(SDIRS)
    return pl.pallas_call(
        kernel,
        out_shape=jax.ShapeDtypeStruct(observed.shape, F32),
        in_specs=[hbm, smem, vmem, vmem, smem, vmem],
        out_specs=hbm,
        scratch_shapes=[
            pltpu.VMEM((EX, EZ, NY), F32), pltpu.VMEM((EX, EZ, NY), F32),
            pltpu.VMEM((EX, NZ, NY), F32), pltpu.VMEM((EX, NZ, NY), F32),
            pltpu.VMEM((4, NZ, 128), F32), pltpu.VMEM((4, 4, 8, 128), F32),
            pltpu.VMEM((2, EZ, 128), F32), pltpu.VMEM((2, EZ, 128), F32),
            pltpu.VMEM((2, NZ, 128), F32), pltpu.VMEM((2, NZ, 128), F32),
            pltpu.VMEM((2, 2, 3, 8, 128), F32), pltpu.VMEM((2, 2, 3, 8, 128), F32),
            pltpu.VMEM((2, 2, 3, 8, 128), F32), pltpu.VMEM((2, 2, 3, 8, 128), F32),
            pltpu.VMEM((2, EZ, 128), F32),
            pltpu.VMEM((NX, EZ, NY), F32), pltpu.VMEM((NX, NZ, NY), F32), pltpu.VMEM((NX, NZ, NY), F32),
            pltpu.VMEM((8, 128), F32), pltpu.VMEM((EZ, 128), F32), pltpu.VMEM((14, EZ, 128), F32),
            pltpu.VMEM((3, 256, 256), BF16),
            dma((NX,)), dma((NX,)), dma((2, 2)),
            dma((ne,)), dma((ne,)), dma((ne,)), dma((ne,)),
            dma((ns,)), dma((ns,)), dma((ns,)), dma((ns,)),
        ],
        compiler_params=pltpu.CompilerParams(collective_id=0, has_side_effects=True, vmem_limit_bytes=40 * 1024 * 1024),
        name="deconvolve",
    )(observed, zone_of_slice, lateral_x, lateral_y, depth_psf, stitch_width)


def solution(mesh):
    in_specs = (P("gz", "sx", "sy"), P("gz"), P(), P(), P(), P())
    out_specs = P("gz", "sx", "sy")
    return jax.shard_map(body, mesh=mesh, in_specs=in_specs, out_specs=out_specs, check_vma=False)
```

time: 52.8 us -> 44.3 us (0.84); the launches traced: 52.6 us -> 43.5 us
  Pallas kernels: 49.9 us -> 40.7 us
    pallas_call x1, Pallas kernels: 49.9 us -> 40.7 us  [body(): pl.pallas_call(kernel, out_shape=jax.ShapeDtypeStruct(observed.shape, F32...]
where the time goes in v1:
time: 44.3 us; the launch traced here: 43.5 us
  Pallas kernels  40.7 us (92%)
  local copies, waits for them, and re-layouts  2.68 us (6%)
    pallas_call x1, Pallas kernels, body(): pl.pallas_call(kernel, out_shape=jax.ShapeDtypeStruct(observed.shape, F32...  40.7 us
    unnamed x12, local copies, waits for them, and re-layouts  2.68 us

profile of v1, /device:TPU:2, one launch (start us, length us, event | category | flops | bytes accessed | tf_op | source)
XLA Modules:
  0.0 43.5 jit_solution(18316544545649710955)
XLA Ops:
  0.0 0.0 copy-start.4
  0.0 0.0 copy-start.2
  0.0 0.0 copy-start.1
  0.0 0.0 copy-start.3
  0.0 0.8 %copy.7.stitch = s32[4,4,2]{2,1,0:T(4,128)S(1)} copy(s32[4,4,2]{1,2,0:T(2,128)} %param.11) | data formatting | bytes 256 | tf_op args[5]
  0.9 0.0 copy-done.4
  0.9 0.0 copy-done.2
  0.9 0.0 copy-done.1
  0.9 0.0 copy-done.3
  0.9 0.0 copy-start
  0.9 1.0 %copy-done = f32[64,16,128]{2,1,0:T(8,128)S(1)} copy-done((f32[64,16,128]{2,1,0:T(8,128)S(1)}, f32[64,16,128]{2,1,0:T(8,128)}, u32[]{:S(2)}) %copy-start) | copy-done | bytes 524312
  1.9 40.7 %deconvolve.1 = f32[64,16,128]{2,1,0:T(8,128)S(1)} custom-call(f32[64,16,128]{2,1,0:T(8,128)S(1)} %copy-done, s32[64]{0:T(128)S(1)} %copy-done.3, f32[8,7]{1,0:T(8,128)S(1)} %copy-done.1, f32[8,7]{1,0:T(8,128)S(1)} %copy-done.2, f32[17]{0:T(128)S(1)} %copy-done.4, s32[4,4,2]{2,1,0:T(4,128)S(1)} %copy.7.stitch), custom_call_target="tpu_custom_call" | custom-call | tf_op jit(solution)/shard_map/deconvolve/pallas_call | solution.py:385
  42.7 0.8 %copy.9 = f32[64,16,128]{2,1,0:T(8,128)} copy(f32[64,16,128]{2,1,0:T(8,128)S(1)} %deconvolve.1) | data formatting | bytes 1048576
Async XLA Ops:
  0.0 0.9 %copy-start.4 = (f32[17]{0:T(128)S(1)}, f32[17]{0:T(128)}, u32[]{:S(2)}) copy-start(f32[17]{0:T(128)} %psf.1) | copy-start | bytes 208
  0.0 0.9 %copy-start.2 = (f32[8,7]{1,0:T(8,128)S(1)}, f32[8,7]{1,0:T(8,128)}, u32[]{:S(2)}) copy-start(f32[8,7]{1,0:T(8,128)} %lat_y.1) | copy-start | bytes 676
  0.0 0.9 %copy-start.1 = (f32[8,7]{1,0:T(8,128)S(1)}, f32[8,7]{1,0:T(8,128)}, u32[]{:S(2)}) copy-start(f32[8,7]{1,0:T(8,128)} %lat_x.1) | copy-start | bytes 676
  0.0 0.9 %copy-start.3 = (s32[64]{0:T(128)S(1)}, s32[64]{0:T(128)}, u32[]{:S(2)}) copy-start(s32[64]{0:T(128)} %zone.1) | copy-start | bytes 772
  0.9 1.0 %copy-start = (f32[64,16,128]{2,1,0:T(8,128)S(1)}, f32[64,16,128]{2,1,0:T(8,128)}, u32[]{:S(2)}) copy-start(f32[64,16,128]{2,1,0:T(8,128)} %obs.1) | copy-start | bytes 1572868

commit v2 on v1

--- a/solution.py
+++ b/solution.py
@@ -18,6 +18,7 @@
 DIRS = [d for d in itertools.product((-1, 0, 1), repeat=3) if d != (0, 0, 0)]
 SDIRS = [d for d in DIRS if d[2] == 0]
 KX, KY = 0, 7
+UNROLL = 4
 PAIRS = ((0, 1), (2, 4), (5, 6))
 CORNERS = {(1, 1): (78, 110), (1, -1): (81, 113), (-1, 1): (0, 96), (-1, -1): (3, 99)}
 
@@ -25,7 +26,7 @@
 def kernel(
     obs, zone, lat_x, lat_y, psf, stitch, out,
     est1, est2, spr1, spr2, pk, qk, ye1, ye2, ys1, ys2, qe1, qe2, qs1, qs2, ch, lest, rnorm, res,
-    ktab, taps, tb, smat, in_sem, out_sem, t_sem,
+    ktab, taps, tb, smat, scr, in_sem, out_sem, t_sem,
     es1, er1, es2, er2, ss1, sr1, ss2, sr2,
 ):
     sx, sy, gz = lax.axis_index("sx"), lax.axis_index("sy"), lax.axis_index("gz")
@@ -161,10 +162,13 @@
             guarded(inside(sign * dx, sign * dy), go)
 
     def lateral(rows_of, strips_of, flip, sink, lo, hi, off):
-        def body(g, _):
+        def taps_at(g):
             trow = pl.ds(pl.multiple_of(g * 8 + off, 8), 8)
-            kx = [tb[KX + (6 - a if flip else a), trow, :] for a in range(7)]
-            ky = [tb[KY + (6 - b if flip else b), trow, :] for b in range(7)]
+            return ([tb[KX + (6 - a if flip else a), trow, :] for a in range(7)],
+                    [tb[KY + (6 - b if flip else b), trow, :] for b in range(7)])
+
+        for g in range(lo, hi):
+            kx, ky = taps_at(g)
             c, c1, c2 = strips_of(g)
             c1, c2 = jnp.where(lane < 96, c, c1), jnp.where(lane < 96, c, c2)
             al = kx[3] * c
@@ -175,6 +179,11 @@
                 ok = {0: lane6 >= 3, 1: jnp.logical_or(lane6 == 3, lane6 == 4), 2: lane6 == 3,
                       4: lane6 == 2, 5: jnp.logical_or(lane6 == 1, lane6 == 2), 6: lane6 <= 2}[b]
                 sc = sc + jnp.where(ok, ky[b] * pltpu.roll(al, (R - b) % 128, 1), 0.0)
+            scr[8 * g : 8 * g + 8, :] = sc
+
+        def group(g):
+            kx, ky = taps_at(g)
+            sc = scr[pl.ds(pl.multiple_of(g * 8, 8), 8), :]
             window = [rows_of(x, g) for x in range(6)]
             along = []
             for x in range(NX):
@@ -185,18 +194,19 @@
                 along.append(v)
             hi, lo = split3(jnp.concatenate(along, axis=0))
             both = jnp.concatenate([hi, lo], axis=1)
-            acc = [ky[R] * v for v in along]
+            acc = [ky[R] * v + jnp.where(edge, pltpu.roll(sc, (-(6 * x + R)) % 128, 1), 0.0) for x, v in enumerate(along)]
             for n, (b0, b1) in enumerate(PAIRS):
                 moved = jnp.dot(both, smat[n], preferred_element_type=F32)
                 for x in range(NX):
                     acc[x] = acc[x] + ky[b0] * moved[8 * x : 8 * x + 8, 0:128] + ky[b1] * moved[8 * x : 8 * x + 8, 128:256]
-            done = []
-            for x in range(NX):
-                done.append(acc[x] + jnp.where(edge, pltpu.roll(sc, (-(6 * x + R)) % 128, 1), 0.0))
-            sink(g, done)
+            sink(g, acc)
+
+        def body(i, _):
+            for k in range(UNROLL):
+                group(lo + i * UNROLL + k)
             return 0
 
-        lax.fori_loop(lo, hi, body, 0)
+        lax.fori_loop(0, (hi - lo) // UNROLL, body, 0)
 
     def rows_from(ref):
         return lambda x, g: ref[x, pl.ds(pl.multiple_of(g * 8, 8), 8), :]
@@ -398,7 +408,7 @@
             pltpu.VMEM((2, EZ, 128), F32),
             pltpu.VMEM((NX, EZ, NY), F32), pltpu.VMEM((NX, NZ, NY), F32), pltpu.VMEM((NX, NZ, NY), F32),
             pltpu.VMEM((8, 128), F32), pltpu.VMEM((EZ, 128), F32), pltpu.VMEM((14, EZ, 128), F32),
-            pltpu.VMEM((3, 256, 256), BF16),
+            pltpu.VMEM((3, 256, 256), BF16), pltpu.VMEM((EZ, 128), F32),
             dma((NX,)), dma((NX,)), dma((2, 2)),
             dma((ne,)), dma((ne,)), dma((ne,)), dma((ne,)),
             dma((ns,)), dma((ns,)), dma((ns,)), dma((ns,)),

time: 44.3 us -> 38.4 us (0.87)
  the two profiles are of different devices: /device:TPU:2 before, /device:TPU:1 now
where the time goes in v2:
time: 38.4 us; the launch traced here: 38.3 us
  Pallas kernels  35.5 us (92%)
  local copies, waits for them, and re-layouts  2.68 us (7%)
    pallas_call x1, Pallas kernels, body(): pl.pallas_call(kernel, out_shape=jax.ShapeDtypeStruct(observed.shape, F32...  35.5 us
    unnamed x12, local copies, waits for them, and re-layouts  2.68 us

profile of v2, /device:TPU:1, one launch (start us, length us, event | category | flops | bytes accessed | tf_op | source)
XLA Modules:
  0.0 38.3 jit_solution(17650963077225263342)
XLA Ops:
  0.0 0.0 copy-start.4
  0.0 0.0 copy-start.2
  0.0 0.0 copy-start.1
  0.0 0.0 copy-start.3
  0.0 0.8 %copy.7.stitch = s32[4,4,2]{2,1,0:T(4,128)S(1)} copy(s32[4,4,2]{1,2,0:T(2,128)} %param.11) | data formatting | bytes 256 | tf_op args[5]
  0.9 0.0 copy-done.4
  0.9 0.0 copy-done.2
  0.9 0.0 copy-done.1
  0.9 0.0 copy-done.3
  0.9 0.0 copy-start
  0.9 1.0 %copy-done = f32[64,16,128]{2,1,0:T(8,128)S(1)} copy-done((f32[64,16,128]{2,1,0:T(8,128)S(1)}, f32[64,16,128]{2,1,0:T(8,128)}, u32[]{:S(2)}) %copy-start) | copy-done | bytes 524312
  1.9 35.5 %deconvolve.1 = f32[64,16,128]{2,1,0:T(8,128)S(1)} custom-call(f32[64,16,128]{2,1,0:T(8,128)S(1)} %copy-done, s32[64]{0:T(128)S(1)} %copy-done.3, f32[8,7]{1,0:T(8,128)S(1)} %copy-done.1, f32[8,7]{1,0:T(8,128)S(1)} %copy-done.2, f32[17]{0:T(128)S(1)} %copy-done.4, s32[4,4,2]{2,1,0:T(4,128)S(1)} %copy.7.stitch), custom_call_target="tpu_custom_call" | custom-call | tf_op jit(solution)/shard_map/deconvolve/pallas_call | solution.py:395
  37.5 0.8 %copy.9 = f32[64,16,128]{2,1,0:T(8,128)} copy(f32[64,16,128]{2,1,0:T(8,128)S(1)} %deconvolve.1) | data formatting | bytes 1048576
Async XLA Ops:
  0.0 0.9 %copy-start.4 = (f32[17]{0:T(128)S(1)}, f32[17]{0:T(128)}, u32[]{:S(2)}) copy-start(f32[17]{0:T(128)} %psf.1) | copy-start | bytes 208
  0.0 0.9 %copy-start.2 = (f32[8,7]{1,0:T(8,128)S(1)}, f32[8,7]{1,0:T(8,128)}, u32[]{:S(2)}) copy-start(f32[8,7]{1,0:T(8,128)} %lat_y.1) | copy-start | bytes 676
  0.0 0.9 %copy-start.1 = (f32[8,7]{1,0:T(8,128)S(1)}, f32[8,7]{1,0:T(8,128)}, u32[]{:S(2)}) copy-start(f32[8,7]{1,0:T(8,128)} %lat_x.1) | copy-start | bytes 676
  0.0 0.9 %copy-start.3 = (s32[64]{0:T(128)S(1)}, s32[64]{0:T(128)}, u32[]{:S(2)}) copy-start(s32[64]{0:T(128)} %zone.1) | copy-start | bytes 772
  0.9 1.0 %copy-start = (f32[64,16,128]{2,1,0:T(8,128)S(1)}, f32[64,16,128]{2,1,0:T(8,128)}, u32[]{:S(2)}) copy-start(f32[64,16,128]{2,1,0:T(8,128)} %obs.1) | copy-start | bytes 1572868

commit v3 on v1

v3 whole, which is shorter than its diff:
```python
import itertools
import jax
import jax.numpy as jnp
from jax import lax
from jax.experimental import pallas as pl
from jax.experimental.pallas import tpu as pltpu
from jax.sharding import PartitionSpec as P

MESH = pl.DeviceIdType.MESH
F32 = jnp.float32
BF16 = jnp.bfloat16
NX, NY, NZ = 16, 128, 64
R = 3
HZ = 16
EZ = NZ + 2 * HZ
EX = NX + 2 * R
SX, SY, GZ = 4, 4, 8
DIRS = [d for d in itertools.product((-1, 0, 1), repeat=3) if d != (0, 0, 0)]
DIRS += [(1, 0, 2), (-1, 0, 2)]
SDIRS = [d for d in DIRS if d[2] in (0, 2)]
KX, KY, KF, KB = 0, 7, 14, 20
EDGE = (0, 1, 2, 13, 14, 15)
INNER = tuple(range(3, 13))
PAIRS = ((0, 1), (2, 4), (5, 6))
CORNERS = {(1, 1): (78, 110), (1, -1): (81, 113), (-1, 1): (0, 96), (-1, -1): (3, 99)}


def kernel(
    obs, zone, lat_x, lat_y, psf, stitch, out,
    est1, est2, spr1, spr2, pk, qk, ye1, ye2, ys1, ys2, qe1, qe2, qs1, qs2, ch, lest, rnorm, res,
    ktab, taps, tb, smat, scr, pmain, pnorm, in_sem, out_sem, t_sem,
    es1, er1, es2, er2, ss1, sr1, ss2, sr2,
):
    sx, sy, gz = lax.axis_index("sx"), lax.axis_index("sy"), lax.axis_index("gz")
    lane = lax.broadcasted_iota(jnp.int32, (8, 128), 1)
    lane6 = lane % 6
    edge = jnp.logical_or(lane < R, lane >= NY - R)
    lane_all = lax.broadcasted_iota(jnp.int32, (EZ, 128), 1)
    edge_all = jnp.logical_or(lane_all < R, lane_all >= NY - R)

    loads = [pltpu.make_async_copy(obs.at[:, x, :], est1.at[R + x, pl.ds(HZ, NZ)], in_sem.at[x]) for x in range(NX)]
    for c in loads:
        c.start()

    def inside(dx, dy):
        ok = None
        for at, d, n in ((sx, dx, SX), (sy, dy, SY)):
            if d:
                t = at < n - 1 if d > 0 else at > 0
                ok = t if ok is None else jnp.logical_and(ok, t)
        return ok

    def guarded(cond, fn):
        if cond is None:
            fn()
        else:
            pl.when(cond)(fn)

    def device(dx, dy, dz):
        return (sx + dx, sy + dy, lax.rem(gz + dz + GZ, GZ))

    for dx, slot, rows in ((1, 0, 0), (-1, 1, EX - R)):
        @pl.when(jnp.logical_not(inside(-dx, 0)))
        def _(slot=slot, rows=rows):
            for e in (est1, est2, spr1, spr2):
                e[pl.ds(rows, R)] = jnp.zeros((R,) + e.shape[1:], F32)
            for q in (qe1, qe2, qs1, qs2):
                for side in range(2):
                    q[side, slot] = jnp.zeros(q.shape[2:], F32)
    for dy, side in ((1, 0), (-1, 1)):
        @pl.when(jnp.logical_not(inside(0, -dy)))
        def _(side=side):
            for y in (ye1, ye2, ys1, ys2, qe1, qe2, qs1, qs2):
                y[side] = jnp.zeros(y.shape[1:], F32)

    barrier = pltpu.get_barrier_semaphore()
    for dx, dy in itertools.product((-1, 0, 1), repeat=2):
        def greet(dx=dx, dy=dy):
            for dz in (-1, 0, 1):
                if (dx, dy, dz) != (0, 0, 0):
                    pl.semaphore_signal(barrier, inc=1, device_id=device(dx, dy, dz), device_id_type=MESH)
        guarded(inside(dx, dy), greet)

    def make_taps(g, _):
        rows = pl.ds(pl.multiple_of(g * 8, 8), 8)
        t = taps[rows, :]
        for i in range(14):
            tb[i, rows, :] = jnp.broadcast_to(t[:, i : i + 1], (8, 128))
        for k, b in enumerate((0, 1, 2, 4, 5, 6)):
            ok = {0: lane6 >= 3, 1: jnp.logical_or(lane6 == 3, lane6 == 4), 2: lane6 == 3,
                  4: lane6 == 2, 5: jnp.logical_or(lane6 == 1, lane6 == 2), 6: lane6 <= 2}[b]
            tb[KF + k, rows, :] = jnp.where(ok, jnp.broadcast_to(t[:, 7 + b : 8 + b], (8, 128)), 0.0)
            tb[KB + k, rows, :] = jnp.where(ok, jnp.broadcast_to(t[:, 13 - b : 14 - b], (8, 128)), 0.0)
        return 0


    def place(acc, v, x):
        at = jnp.logical_and(lane >= 6 * x, lane < 6 * x + 6)
        return jnp.where(at, pltpu.roll(v, 6 * x + R, 1), acc)

    def pack_block(src, off, dst):
        for g in range(NZ // 8):
            acc = jnp.zeros((8, 128), F32)
            for x in range(NX):
                acc = place(acc, src[R + x, g * 8 + off : g * 8 + off + 8, :], x)
            dst[g * 8 : g * 8 + 8, :] = acc

    def pack_corners(groups, dst):
        for k, (first, _) in enumerate(CORNERS.values()):
            acc = jnp.zeros((8, 128), F32)
            for g in range(NZ // 8):
                at = jnp.logical_and(lane >= 16 * g, lane < 16 * g + 16)
                acc = jnp.where(at, pltpu.roll(groups[g], (16 * g - first) % 128, 1), acc)
            dst[k] = acc

    def unpack_corners(src, halo):
        up = (lane + 4) % 6 < R
        for g in range((NZ + 2 * halo) // 8):
            slot, local = 1, g - halo // 8
            if local < 0:
                slot, local = 0, local + NZ // 8
            elif local >= NZ // 8:
                slot, local = 2, local - NZ // 8
            got = [pltpu.roll(src[0 if d[1] > 0 else 1, 0 if d[0] > 0 else 1, slot], (at - 16 * local) % 128, 1)
                   for d, (_, at) in CORNERS.items()]
            cu = jnp.where(up, got[0], got[1])
            cd = jnp.where(left, got[2], got[3])
            ch[0, g * 8 : g * 8 + 8, :] = jnp.where(lane < 110, cd, cu)
            ch[1, g * 8 : g * 8 + 8, :] = cd

    def copies(main, strips, packed, corners, cpacked, halo, dirs, send, recv):
        found = {}
        for i, (dx, dy, dz) in enumerate(dirs):
            zs, zd, n = {0: (0, halo, NZ), 1: (NZ - HZ, 0, HZ), -1: (0, halo + NZ, HZ), 2: (NZ // 2, halo + NZ // 2, NZ // 2)}[dz]
            if dx and not dy and dz == 0:
                n = NZ // 2
            if dy == 0:
                xs, xd, m = {0: (R, R, NX), 1: (NX, 0, R), -1: (R, R + NX, R)}[dx]
                src = main.at[pl.ds(xs, m), pl.ds(halo + zs, n), :]
                dst = main.at[pl.ds(xd, m), pl.ds(zd, n), :]
            elif dx == 0:
                src = packed.at[pl.ds(zs, n), :]
                dst = strips.at[0 if dy > 0 else 1, pl.ds(zd, n), :]
            else:
                src = cpacked.at[list(CORNERS).index((dx, dy))]
                dst = corners.at[0 if dy > 0 else 1, 0 if dx > 0 else 1, 1 - dz]
            found[(dx, dy, dz)] = pltpu.make_async_remote_copy(
                src_ref=src, dst_ref=dst, send_sem=send.at[i], recv_sem=recv.at[i],
                device_id=device(dx, dy, 0 if dz == 2 else dz), device_id_type=MESH)
        return found

    X_LOW, X_HIGH = [(1, 0, 0), (-1, 0, 0)], [(1, 0, 2), (-1, 0, 2)]
    X_FACE, Z_FACE, Y_FACE = X_LOW + X_HIGH, [(0, 0, 1), (0, 0, -1)], [(0, 1, 0), (0, -1, 0)]
    XZ = [(dx, 0, dz) for dx in (1, -1) for dz in (1, -1)]
    YZ = [(0, dy, dz) for dy in (1, -1) for dz in (1, -1)]
    CORN = [(dx, dy, dz) for dx in (1, -1) for dy in (1, -1) for dz in (0, 1, -1)]
    XS = XZ + X_LOW + X_HIGH
    SIDES = [(0, dy, dz) for dy in (1, -1) for dz in (1, -1, 0)]

    def each(found, sign, what, which):
        for (dx, dy), ds in itertools.groupby([d for d in which if d in found], key=lambda d: d[:2]):
            def go(ds=tuple(ds)):
                for d in ds:
                    getattr(found[d], what)()
            guarded(inside(sign * dx, sign * dy), go)

    def taps_at(g, flip, off):
        trow = pl.ds(pl.multiple_of(g * 8 + off, 8), 8)
        return ([tb[KX + (6 - a if flip else a), trow, :] for a in range(7)],
                [tb[KY + (6 - b if flip else b), trow, :] for b in range(7)])

    def halo_strips(c, c1, c2, flip, off):
        n = c.shape[0]
        rows = slice(off, off + n)
        own = lane_all[:n] < 96
        c1, c2 = jnp.where(own, c, c1), jnp.where(own, c, c2)
        al = tb[KX + 3, rows, :] * c
        for a in (0, 1, 2, 4, 5, 6):
            al = al + tb[KX + (6 - a if flip else a), rows, :] * pltpu.roll(c2 if a == 6 else c1, (18 - 6 * a) % 128, 1)
        sc = None
        for k, b in enumerate((0, 1, 2, 4, 5, 6)):
            v = tb[(KB if flip else KF) + k, rows, :] * pltpu.roll(al, (R - b) % 128, 1)
            sc = v if sc is None else sc + v
        scr[0:n, :] = sc

    def conv(rows_of, flip, xs, lo, hi, off, fuse, unroll, sink):
        def part(first):
            groups = [first + k for k in range(fuse)]
            along, taps_y = [], []
            for g in groups:
                kx, ky = taps_at(g, flip, off)
                taps_y.append(ky)
                rows = {}
                for x in xs:
                    for a in range(7):
                        if x + a not in rows:
                            rows[x + a] = rows_of(x + a, g)
                    v = kx[0] * rows[x]
                    for a in range(1, 7):
                        v = v + kx[a] * rows[x + a]
                    along.append(v)
            hi, lo_ = split3(jnp.concatenate(along, axis=0))
            both = jnp.concatenate([hi, lo_], axis=1)
            n = len(xs)
            acc = [taps_y[k // n][R] * v for k, v in enumerate(along)]
            for m, (b0, b1) in enumerate(PAIRS):
                moved = jnp.dot(both, smat[m], preferred_element_type=F32)
                for k in range(len(acc)):
                    ky = taps_y[k // n]
                    acc[k] = acc[k] + ky[b0] * moved[8 * k : 8 * k + 8, 0:128] + ky[b1] * moved[8 * k : 8 * k + 8, 128:256]
            for k, g in enumerate(groups):
                sink(g, xs, acc[k * n : k * n + n])

        def body(i, _):
            for k in range(unroll):
                part(lo + (i * unroll + k) * fuse)
            return 0

        lax.fori_loop(0, (hi - lo) // (fuse * unroll), body, 0)

    def spread_strip(v, x):
        return jnp.where(edge if v.shape[0] == 8 else edge_all[: v.shape[0]], pltpu.roll(v, (-(6 * x + R)) % 128, 1), 0.0)

    def rows_from(ref):
        return lambda x, g: ref[x, pl.ds(pl.multiple_of(g * 8, 8), 8), :]

    left = lane6 < R

    def strips_from(ref):
        n = ref.shape[1]
        return jnp.where(lane_all[:n] % 6 < R, ref[0], ref[1]), ch[0, 0:n, :], ch[1, 0:n, :]

    def band(i, j, k):
        row = stitch[pl.ds(jnp.clip(sx + i, 0, SX - 1), 1)][0, k : k + 1, :].astype(F32)
        at = lax.broadcasted_iota(jnp.int32, (1, SY), 1) == jnp.clip(sy + j, 0, SY - 1)
        return jnp.broadcast_to(jnp.sum(jnp.where(at, row, 0.0), axis=1, keepdims=True), (8, 128))

    def half(pos, width):
        return jnp.where(pos.astype(F32) < width, 0.5, 1.0).astype(F32)

    bands = {(i, j): (band(i, j, 0), band(i, j, 1)) for i in (-1, 0, 1) for j in (-1, 0, 1)}
    wrows = []
    for x in range(-R, NX + R):
        i = -1 if x < 0 else (1 if x >= NX else 0)
        row = half(jnp.full((8, 128), x - i * NX, jnp.int32), bands[i, 0][0]) * half(lane, bands[i, 0][1])
        cond = inside(i, 0)
        if cond is not None:
            row = row * jnp.where(cond, 1.0, 0.0).astype(F32)
        wrows.append(row)
    wpos = {0: lane // 6, -1: NX - R + (lane - 110) // 6, 1: (lane - 96) // 6}
    wstrips = []
    for i in (0, -1, 1):
        lane_i = (lane + 4) % 6 if i < 0 else lane6
        parts = []
        for j, pos in ((-1, NY - R + lane_i), (1, lane_i - R)):
            v = half(wpos[i], bands[i, j][0]) * half(pos, bands[i, j][1])
            parts.append(v * jnp.where(inside(i, j), 1.0, 0.0).astype(F32))
        wstrips.append(jnp.where(lane_i < R, parts[0], parts[1]))
    wstrips_at = (wstrips[0], jnp.where(lane < 110, wstrips[2], wstrips[1]), wstrips[2])

    total = psf[0]
    for j in range(1, 17):
        total = total + psf[j]

    def depth_matrix(m, k, forward):
        off = lax.broadcasted_iota(jnp.int32, (m, k), 1) - lax.broadcasted_iota(jnp.int32, (m, k), 0)
        h = jnp.zeros((m, k), F32)
        for j in range(17):
            h = jnp.where(off == j, psf[16 - j if forward else j], h)
        h = h / jnp.full((m, k), total, F32)
        hi = h.astype(BF16)
        lo = (h - hi.astype(F32)).astype(BF16)
        return jnp.concatenate([hi, hi, lo], axis=1)

    def split3(v):
        hi = v.astype(BF16)
        lo = (v - hi.astype(F32)).astype(BF16)
        return hi, lo

    nx = 3 - (sx == 0).astype(jnp.int32) - (sx == SX - 1).astype(jnp.int32)
    ny = 3 - (sy == 0).astype(jnp.int32) - (sy == SY - 1).astype(jnp.int32)
    for c in loads:
        c.wait()
    pl.semaphore_wait(barrier, nx * ny * 3 - 1)

    tcopies = [
        pltpu.make_async_remote_copy(
            src_ref=taps.at[pl.ds(s, HZ), :], dst_ref=taps.at[pl.ds(d, HZ), :],
            send_sem=t_sem.at[0, i], recv_sem=t_sem.at[1, i], device_id=device(0, 0, dz), device_id_type=MESH)
        for i, (dz, s, d) in enumerate(((1, NZ, 0), (-1, HZ, HZ + NZ)))
    ]
    e1 = copies(est1, ye1, pk.at[0], qe1, qk.at[0], HZ, DIRS, es1, er1)
    s1 = copies(spr1, ys1, pk.at[1], qs1, qk.at[1], 0, SDIRS, ss1, sr1)
    e2 = copies(est2, ye2, pk.at[2], qe2, qk.at[2], HZ, DIRS, es2, er2)
    s2 = copies(spr2, ys2, pk.at[3], qs2, qk.at[3], 0, SDIRS, ss2, sr2)

    def packed_groups(k):
        return [pk[k, 8 * g : 8 * g + 8, :] for g in range(NZ // 8)]

    each(e1, 1, "start", XS + Z_FACE)
    pack_block(est1, HZ, pk.at[0])
    pack_corners(packed_groups(0), qk.at[0])
    each(e1, 1, "start", CORN + SIDES)

    ktab[...] = jnp.zeros((8, 128), F32)
    ktab[:, 0:7] = lat_x[...]
    ktab[:, 7:14] = lat_y[...]
    for z in range(NZ):
        taps[HZ + z : HZ + z + 1, :] = ktab[pl.ds(zone[z], 1), :]
    for c in tcopies:
        c.start()

    row = lax.broadcasted_iota(jnp.int32, (256, 128), 0) % 128
    col = lax.broadcasted_iota(jnp.int32, (256, 128), 1)
    for n, pair in enumerate(PAIRS):
        for k, b in enumerate(pair):
            smat[n, :, 128 * k : 128 * k + 128] = jnp.where(row == col + (b - R), 1.0, 0.0).astype(BF16)
    lax.fori_loop(2, 10, make_taps, 0)

    def reciprocal(v):
        r = pltpu.reciprocal(v, approx=True)
        return r * (2.0 - v * r)

    def rows8(g, off=0):
        return pl.ds(pl.multiple_of(g * 8 + off, 8), 8)

    def keep_norm(g, xs, values):
        sc = scr[rows8(g), :]
        acc = jnp.zeros((8, 128), F32)
        for x, v in zip(xs, values):
            r = reciprocal(v + spread_strip(sc, x))
            rnorm[x, rows8(g), :] = r
            acc = place(acc, r, x)
        pnorm[rows8(g), :] = acc

    def keep_lest(g, xs, values):
        for x, v in zip(xs, values):
            lest[x, rows8(g), :] = v

    def keep_update(g, xs, values):
        acc = pmain[rows8(g), :]
        for x, v in zip(xs, values):
            lest[x, rows8(g), :] = v
            acc = place(acc, v, x)
        pmain[rows8(g), :] = acc

    halo_strips(*[jnp.concatenate([v] * (NZ // 8), axis=0) for v in wstrips_at], True, HZ)
    conv(lambda x, g: wrows[x], True, tuple(range(NX)), 0, NZ // 8, HZ, 1, 4, keep_norm)
    conv(rows_from(est1), False, INNER, 2, 10, 0, 2, 2, keep_lest)
    fwd1 = depth_matrix(48, 64, True)
    fwd2 = depth_matrix(32, 48, True)
    bwd = depth_matrix(64, 80, False)
    for c in tcopies:
        c.wait_recv()
    for g in (0, 1, 10, 11):
        make_taps(g, 0)

    def depth(part, spr, strip):
        blurs = []
        for a, b in part:
            pair = jnp.concatenate([lest[x] + spread_strip(scr[...], x) for x in (a, b)], axis=1)
            hi, lo = split3(pair)
            top = jnp.concatenate([hi[0:64], lo[0:64], hi[0:64]], axis=0)
            low = jnp.concatenate([hi[48:96], lo[48:96], hi[48:96]], axis=0)
            blurs.append(jnp.concatenate(
                [jnp.dot(fwd1, top, preferred_element_type=F32), jnp.dot(fwd2, low, preferred_element_type=F32)], axis=0))
        for (a, b), blur in zip(part, blurs):
            wide = jnp.concatenate([wrows[R + a][0:1], wrows[R + b][0:1]], axis=1)
            seen = jnp.concatenate([est1[R + a, 8:88, :], est1[R + b, 8:88, :]], axis=1)
            hi, lo = split3(wide * seen * reciprocal(blur))
            back = jnp.dot(bwd, jnp.concatenate([hi, lo, hi], axis=0), preferred_element_type=F32)
            for x, v in ((a, back[:, 0:128]), (b, back[:, 128:256])):
                spr[R + x] = v
                strip = [place(t, v[8 * g : 8 * g + 8], x) for g, t in enumerate(strip)]
        return strip

    for est, ye, qe, ecop, spr, ys, qs, scop, pks, last in (
        (est1, ye1, qe1, e1, spr1, ys1, qs1, s1, 1, False),
        (est2, ye2, qe2, e2, spr2, ys2, qs2, s2, 3, True),
    ):
        if last:
            conv(rows_from(est), False, INNER, 2, 10, 0, 2, 2, keep_lest)
        each(ecop, -1, "wait_recv", Z_FACE)
        conv(rows_from(est), False, INNER, 0, 2, 0, 2, 1, keep_lest)
        conv(rows_from(est), False, INNER, 10, 12, 0, 2, 1, keep_lest)
        each(ecop, -1, "wait_recv", XZ + X_LOW)
        conv(rows_from(est), False, EDGE, 0, 6, 0, 2, 3, keep_lest)
        each(ecop, -1, "wait_recv", X_HIGH)
        conv(rows_from(est), False, EDGE, 6, 12, 0, 2, 3, keep_lest)
        each(ecop, -1, "wait_recv", CORN + SIDES)
        unpack_corners(qe, HZ)
        halo_strips(*strips_from(ye), False, 0)
        strip = [jnp.zeros((8, 128), F32) for _ in range(NZ // 8)]
        strip = depth(((0, 1), (2, 13), (14, 15)), spr, strip)
        each(scop, 1, "start", X_FACE)
        pack_corners(strip, qk.at[pks])
        each(scop, 1, "start", CORN)
        strip = depth(((3, 4), (5, 6), (7, 8), (9, 10), (11, 12)), spr, strip)
        for g, t in enumerate(strip):
            pk[pks, 8 * g : 8 * g + 8, :] = t
        each(scop, 1, "start", Y_FACE)
        pmain[...] = jnp.zeros_like(pmain)
        conv(rows_from(spr), True, INNER, 0, NZ // 8, HZ, 2, 2, keep_update)
        each(scop, -1, "wait_recv", X_LOW)
        conv(rows_from(spr), True, EDGE, 0, 4, HZ, 2, 2, keep_update)
        each(scop, -1, "wait_recv", X_HIGH)
        conv(rows_from(spr), True, EDGE, 4, 8, HZ, 2, 2, keep_update)
        each(scop, -1, "wait_recv", CORN + Y_FACE)
        unpack_corners(qs, 0)
        halo_strips(*strips_from(ys), True, HZ)

        def update(x):
            return est[R + x, HZ : HZ + NZ, :] * (lest[x, 0:NZ, :] + spread_strip(scr[0:NZ, :], x)) * rnorm[x]

        if last:
            for x in range(NX):
                res[x] = update(x)
        else:
            for x in EDGE:
                est2[R + x, HZ : HZ + NZ, :] = update(x)
            each(e2, 1, "start", XS)
            pk[2] = pk[0] * (pmain[...] + scr[0:NZ, :]) * pnorm[...]
            pack_corners(packed_groups(2), qk.at[2])
            for x in INNER:
                est2[R + x, HZ : HZ + NZ, :] = update(x)
            each(e2, 1, "start", Z_FACE + CORN + SIDES)

    stores = [pltpu.make_async_copy(res.at[x], out.at[:, x, :], out_sem.at[x]) for x in range(NX)]
    for c in stores:
        c.start()
    for c in tcopies:
        c.wait_send()
    for found in (e1, s1, e2, s2):
        each(found, 1, "wait_send", XS + Z_FACE + CORN + SIDES)
    for c in stores:
        c.wait()


def body(observed, zone_of_slice, lateral_x, lateral_y, depth_psf, stitch_width):
    hbm = pl.BlockSpec(memory_space=pltpu.HBM)
    smem = pl.BlockSpec(memory_space=pltpu.SMEM)
    vmem = pl.BlockSpec(memory_space=pltpu.VMEM)
    dma = pltpu.SemaphoreType.DMA
    ne, ns = len(DIRS), len(SDIRS)
    return pl.pallas_call(
        kernel,
        out_shape=jax.ShapeDtypeStruct(observed.shape, F32),
        in_specs=[hbm, smem, vmem, vmem, smem, vmem],
        out_specs=hbm,
        scratch_shapes=[
            pltpu.VMEM((EX, EZ, NY), F32), pltpu.VMEM((EX, EZ, NY), F32),
            pltpu.VMEM((EX, NZ, NY), F32), pltpu.VMEM((EX, NZ, NY), F32),
            pltpu.VMEM((4, NZ, 128), F32), pltpu.VMEM((4, 4, 8, 128), F32),
            pltpu.VMEM((2, EZ, 128), F32), pltpu.VMEM((2, EZ, 128), F32),
            pltpu.VMEM((2, NZ, 128), F32), pltpu.VMEM((2, NZ, 128), F32),
            pltpu.VMEM((2, 2, 3, 8, 128), F32), pltpu.VMEM((2, 2, 3, 8, 128), F32),
            pltpu.VMEM((2, 2, 3, 8, 128), F32), pltpu.VMEM((2, 2, 3, 8, 128), F32),
            pltpu.VMEM((2, EZ, 128), F32),
            pltpu.VMEM((NX, EZ, NY), F32), pltpu.VMEM((NX, NZ, NY), F32), pltpu.VMEM((NX, NZ, NY), F32),
            pltpu.VMEM((8, 128), F32), pltpu.VMEM((EZ, 128), F32), pltpu.VMEM((26, EZ, 128), F32),
            pltpu.VMEM((3, 256, 256), BF16), pltpu.VMEM((EZ, 128), F32),
            pltpu.VMEM((NZ, 128), F32), pltpu.VMEM((NZ, 128), F32),
            dma((NX,)), dma((NX,)), dma((2, 2)),
            dma((ne,)), dma((ne,)), dma((ne,)), dma((ne,)),
            dma((ns,)), dma((ns,)), dma((ns,)), dma((ns,)),
        ],
        compiler_params=pltpu.CompilerParams(collective_id=0, has_side_effects=True, vmem_limit_bytes=62800 * 1024),
        name="deconvolve",
    )(observed, zone_of_slice, lateral_x, lateral_y, depth_psf, jnp.swapaxes(stitch_width, 1, 2))


def solution(mesh):
    in_specs = (P("gz", "sx", "sy"), P("gz"), P(), P(), P(), P())
    out_specs = P("gz", "sx", "sy")
    return jax.shard_map(body, mesh=mesh, in_specs=in_specs, out_specs=out_specs, check_vma=False)
```

time: 44.3 us -> 35 us (0.79); the launches traced: 43.5 us -> 34.7 us
  Pallas kernels: 40.7 us -> 32.9 us
  local copies, waits for them, and re-layouts: 2.68 us -> 1.87 us
    pallas_call x1, Pallas kernels: 40.7 us -> 32.9 us  [body(): pl.pallas_call(kernel, out_shape=jax.ShapeDtypeStruct(observed.shape, F32...]
    unnamed x12 -> x1, local copies, waits for them, and re-layouts: 2.68 us -> 1.87 us
where the time goes in v3:
time: 35 us; the launch traced here: 34.7 us
  Pallas kernels  32.9 us (94%)
  local copies, waits for them, and re-layouts  1.87 us (5%)
    pallas_call x1, Pallas kernels, body(): pl.pallas_call(kernel, out_shape=jax.ShapeDtypeStruct(observed.shape, F32...  32.9 us
    unnamed x1, local copies, waits for them, and re-layouts  1.87 us

profile of v3, /device:TPU:2, one launch (start us, length us, event | category | flops | bytes accessed | tf_op | source)
XLA Modules:
  0.0 34.7 jit_solution(13156953520239592492)
XLA Ops:
  0.0 32.9 %deconvolve.1 = f32[64,16,128]{2,1,0:T(8,128)} custom-call(f32[64,16,128]{2,1,0:T(8,128)} %obs.1, s32[64]{0:T(128)} %zone.1, f32[8,7]{1,0:T(8,128)} %lat_x.1, f32[8,7]{1,0:T(8,128)} %lat_y.1, f32[17]{0:T(128)} %psf.1, s32[4,2,4]{2,1,0:T(2,128)} %bitcast.1), custom_call_target="tpu_custom_call" | custom-call | tf_op jit(solution)/shard_map/deconvolve/pallas_call | solution.py:445
  32.9 1.9 %copy.8 = f32[64,16,128]{2,1,0:T(8,128)} copy(f32[64,16,128]{2,1,0:T(8,128)} %deconvolve.1) | data formatting | bytes 1048576

commit v4 on v3

--- a/solution.py
+++ b/solution.py
@@ -16,8 +16,7 @@
 EX = NX + 2 * R
 SX, SY, GZ = 4, 4, 8
 DIRS = [d for d in itertools.product((-1, 0, 1), repeat=3) if d != (0, 0, 0)]
-DIRS += [(1, 0, 2), (-1, 0, 2)]
-SDIRS = [d for d in DIRS if d[2] in (0, 2)]
+SDIRS = [d for d in DIRS if d[2] == 0]
 KX, KY, KF, KB = 0, 7, 14, 20
 EDGE = (0, 1, 2, 13, 14, 15)
 INNER = tuple(range(3, 13))
@@ -37,6 +36,11 @@
     edge = jnp.logical_or(lane < R, lane >= NY - R)
     lane_all = lax.broadcasted_iota(jnp.int32, (EZ, 128), 1)
     edge_all = jnp.logical_or(lane_all < R, lane_all >= NY - R)
+
+    def rows8(g, off=0):
+        if isinstance(g, int):
+            return slice(g * 8 + off, g * 8 + off + 8)
+        return pl.ds(pl.multiple_of(g * 8 + off, 8), 8)
 
     loads = [pltpu.make_async_copy(obs.at[:, x, :], est1.at[R + x, pl.ds(HZ, NZ)], in_sem.at[x]) for x in range(NX)]
     for c in loads:
@@ -82,7 +86,7 @@
         guarded(inside(dx, dy), greet)
 
     def make_taps(g, _):
-        rows = pl.ds(pl.multiple_of(g * 8, 8), 8)
+        rows = rows8(g)
         t = taps[rows, :]
         for i in range(14):
             tb[i, rows, :] = jnp.broadcast_to(t[:, i : i + 1], (8, 128))
@@ -131,9 +135,7 @@
     def copies(main, strips, packed, corners, cpacked, halo, dirs, send, recv):
         found = {}
         for i, (dx, dy, dz) in enumerate(dirs):
-            zs, zd, n = {0: (0, halo, NZ), 1: (NZ - HZ, 0, HZ), -1: (0, halo + NZ, HZ), 2: (NZ // 2, halo + NZ // 2, NZ // 2)}[dz]
-            if dx and not dy and dz == 0:
-                n = NZ // 2
+            zs, zd, n = {0: (0, halo, NZ), 1: (NZ - HZ, 0, HZ), -1: (0, halo + NZ, HZ)}[dz]
             if dy == 0:
                 xs, xd, m = {0: (R, R, NX), 1: (NX, 0, R), -1: (R, R + NX, R)}[dx]
                 src = main.at[pl.ds(xs, m), pl.ds(halo + zs, n), :]
@@ -146,15 +148,14 @@
                 dst = corners.at[0 if dy > 0 else 1, 0 if dx > 0 else 1, 1 - dz]
             found[(dx, dy, dz)] = pltpu.make_async_remote_copy(
                 src_ref=src, dst_ref=dst, send_sem=send.at[i], recv_sem=recv.at[i],
-                device_id=device(dx, dy, 0 if dz == 2 else dz), device_id_type=MESH)
+                device_id=device(dx, dy, dz), device_id_type=MESH)
         return found
 
-    X_LOW, X_HIGH = [(1, 0, 0), (-1, 0, 0)], [(1, 0, 2), (-1, 0, 2)]
-    X_FACE, Z_FACE, Y_FACE = X_LOW + X_HIGH, [(0, 0, 1), (0, 0, -1)], [(0, 1, 0), (0, -1, 0)]
+    X_FACE, Z_FACE, Y_FACE = [(1, 0, 0), (-1, 0, 0)], [(0, 0, 1), (0, 0, -1)], [(0, 1, 0), (0, -1, 0)]
     XZ = [(dx, 0, dz) for dx in (1, -1) for dz in (1, -1)]
     YZ = [(0, dy, dz) for dy in (1, -1) for dz in (1, -1)]
     CORN = [(dx, dy, dz) for dx in (1, -1) for dy in (1, -1) for dz in (0, 1, -1)]
-    XS = XZ + X_LOW + X_HIGH
+    XS = XZ + X_FACE
     SIDES = [(0, dy, dz) for dy in (1, -1) for dz in (1, -1, 0)]
 
     def each(found, sign, what, which):
@@ -165,7 +166,7 @@
             guarded(inside(sign * dx, sign * dy), go)
 
     def taps_at(g, flip, off):
-        trow = pl.ds(pl.multiple_of(g * 8 + off, 8), 8)
+        trow = rows8(g, off)
         return ([tb[KX + (6 - a if flip else a), trow, :] for a in range(7)],
                 [tb[KY + (6 - b if flip else b), trow, :] for b in range(7)])
 
@@ -216,13 +217,16 @@
                 part(lo + (i * unroll + k) * fuse)
             return 0
 
-        lax.fori_loop(0, (hi - lo) // (fuse * unroll), body, 0)
+        if hi - lo == fuse * unroll:
+            body(0, 0)
+        else:
+            lax.fori_loop(0, (hi - lo) // (fuse * unroll), body, 0)
 
     def spread_strip(v, x):
         return jnp.where(edge if v.shape[0] == 8 else edge_all[: v.shape[0]], pltpu.roll(v, (-(6 * x + R)) % 128, 1), 0.0)
 
     def rows_from(ref):
-        return lambda x, g: ref[x, pl.ds(pl.multiple_of(g * 8, 8), 8), :]
+        return lambda x, g: ref[x, rows8(g), :]
 
     left = lane6 < R
 
@@ -231,12 +235,11 @@
         return jnp.where(lane_all[:n] % 6 < R, ref[0], ref[1]), ch[0, 0:n, :], ch[1, 0:n, :]
 
     def band(i, j, k):
-        row = stitch[pl.ds(jnp.clip(sx + i, 0, SX - 1), 1)][0, k : k + 1, :].astype(F32)
-        at = lax.broadcasted_iota(jnp.int32, (1, SY), 1) == jnp.clip(sy + j, 0, SY - 1)
-        return jnp.broadcast_to(jnp.sum(jnp.where(at, row, 0.0), axis=1, keepdims=True), (8, 128))
+        row = stitch[pl.ds(jnp.clip(sx + i, 0, SX - 1), 1), pl.ds(jnp.clip(sy + j, 0, SY - 1), 1), :]
+        return jnp.broadcast_to(row[0, :, k : k + 1], (8, 128))
 
     def half(pos, width):
-        return jnp.where(pos.astype(F32) < width, 0.5, 1.0).astype(F32)
+        return jnp.where(pos < width, 0.5, 1.0).astype(F32)
 
     bands = {(i, j): (band(i, j, 0), band(i, j, 1)) for i in (-1, 0, 1) for j in (-1, 0, 1)}
     wrows = []
@@ -321,9 +324,6 @@
         r = pltpu.reciprocal(v, approx=True)
         return r * (2.0 - v * r)
 
-    def rows8(g, off=0):
-        return pl.ds(pl.multiple_of(g * 8 + off, 8), 8)
-
     def keep_norm(g, xs, values):
         sc = scr[rows8(g), :]
         acc = jnp.zeros((8, 128), F32)
@@ -344,8 +344,6 @@
             acc = place(acc, v, x)
         pmain[rows8(g), :] = acc
 
-    halo_strips(*[jnp.concatenate([v] * (NZ // 8), axis=0) for v in wstrips_at], True, HZ)
-    conv(lambda x, g: wrows[x], True, tuple(range(NX)), 0, NZ // 8, HZ, 1, 4, keep_norm)
     conv(rows_from(est1), False, INNER, 2, 10, 0, 2, 2, keep_lest)
     fwd1 = depth_matrix(48, 64, True)
     fwd2 = depth_matrix(32, 48, True)
@@ -380,34 +378,30 @@
     ):
         if last:
             conv(rows_from(est), False, INNER, 2, 10, 0, 2, 2, keep_lest)
-        each(ecop, -1, "wait_recv", Z_FACE)
-        conv(rows_from(est), False, INNER, 0, 2, 0, 2, 1, keep_lest)
-        conv(rows_from(est), False, INNER, 10, 12, 0, 2, 1, keep_lest)
-        each(ecop, -1, "wait_recv", XZ + X_LOW)
-        conv(rows_from(est), False, EDGE, 0, 6, 0, 2, 3, keep_lest)
-        each(ecop, -1, "wait_recv", X_HIGH)
-        conv(rows_from(est), False, EDGE, 6, 12, 0, 2, 3, keep_lest)
-        each(ecop, -1, "wait_recv", CORN + SIDES)
+        each(ecop, -1, "wait_recv", XZ + X_FACE + Z_FACE + CORN + SIDES)
         unpack_corners(qe, HZ)
         halo_strips(*strips_from(ye), False, 0)
+        conv(rows_from(est), False, EDGE, 0, EZ // 8, 0, 2, 6, keep_lest)
         strip = [jnp.zeros((8, 128), F32) for _ in range(NZ // 8)]
         strip = depth(((0, 1), (2, 13), (14, 15)), spr, strip)
         each(scop, 1, "start", X_FACE)
         pack_corners(strip, qk.at[pks])
         each(scop, 1, "start", CORN)
+        conv(rows_from(est), False, INNER, 0, 2, 0, 2, 1, keep_lest)
+        conv(rows_from(est), False, INNER, 10, 12, 0, 2, 1, keep_lest)
         strip = depth(((3, 4), (5, 6), (7, 8), (9, 10), (11, 12)), spr, strip)
         for g, t in enumerate(strip):
             pk[pks, 8 * g : 8 * g + 8, :] = t
         each(scop, 1, "start", Y_FACE)
         pmain[...] = jnp.zeros_like(pmain)
         conv(rows_from(spr), True, INNER, 0, NZ // 8, HZ, 2, 2, keep_update)
-        each(scop, -1, "wait_recv", X_LOW)
-        conv(rows_from(spr), True, EDGE, 0, 4, HZ, 2, 2, keep_update)
-        each(scop, -1, "wait_recv", X_HIGH)
-        conv(rows_from(spr), True, EDGE, 4, 8, HZ, 2, 2, keep_update)
-        each(scop, -1, "wait_recv", CORN + Y_FACE)
+        if not last:
+            halo_strips(*[jnp.concatenate([v] * (NZ // 8), axis=0) for v in wstrips_at], True, HZ)
+            conv(lambda x, g: wrows[x], True, tuple(range(NX)), 0, NZ // 8, HZ, 1, 4, keep_norm)
+        each(scop, -1, "wait_recv", X_FACE + CORN + Y_FACE)
         unpack_corners(qs, 0)
         halo_strips(*strips_from(ys), True, HZ)
+        conv(rows_from(spr), True, EDGE, 0, NZ // 8, HZ, 2, 4, keep_update)
 
         def update(x):
             return est[R + x, HZ : HZ + NZ, :] * (lest[x, 0:NZ, :] + spread_strip(scr[0:NZ, :], x)) * rnorm[x]
@@ -464,9 +458,9 @@
             dma((ne,)), dma((ne,)), dma((ne,)), dma((ne,)),
             dma((ns,)), dma((ns,)), dma((ns,)), dma((ns,)),
         ],
-        compiler_params=pltpu.CompilerParams(collective_id=0, has_side_effects=True, vmem_limit_bytes=62800 * 1024),
+        compiler_params=pltpu.CompilerParams(collective_id=0, has_side_effects=True, vmem_limit_bytes=54500 * 1024),
         name="deconvolve",
-    )(observed, zone_of_slice, lateral_x, lateral_y, depth_psf, jnp.swapaxes(stitch_width, 1, 2))
+    )(observed, zone_of_slice, lateral_x, lateral_y, depth_psf, stitch_width)
 
 
 def solution(mesh):

time: 35 us -> 32.3 us (0.923); the launches traced: 34.7 us -> 31.7 us
  Pallas kernels: 32.9 us -> 30 us
    pallas_call x1, Pallas kernels: 32.9 us -> 30 us  [body(): pl.pallas_call(kernel, out_shape=jax.ShapeDtypeStruct(observed.shape, F32...]
    unnamed x1 -> x10, local copies, waits for them, and re-layouts: 1.87 us -> 1.65 us
where the time goes in v4:
time: 32.3 us; the launch traced here: 31.7 us
  Pallas kernels  30 us (93%)
  local copies, waits for them, and re-layouts  1.65 us (5%)
    pallas_call x1, Pallas kernels, body(): pl.pallas_call(kernel, out_shape=jax.ShapeDtypeStruct(observed.shape, F32...  30 us
    unnamed x10, local copies, waits for them, and re-layouts  1.65 us

profile of v4, /device:TPU:2, one launch (start us, length us, event | category | flops | bytes accessed | tf_op | source)
XLA Modules:
  0.0 31.7 jit_solution(11999964085284399546)
XLA Ops:
  0.0 0.0 copy-start.3
  0.0 0.0 copy-start.1
  0.0 0.0 copy-start
  0.0 0.0 copy-start.2
  0.0 0.8 %copy.7.stitch = s32[4,4,2]{2,1,0:T(4,128)S(1)} copy(s32[4,4,2]{1,2,0:T(2,128)} %param.11) | data formatting | bytes 256 | tf_op args[5]
  0.9 0.0 copy-done.3
  0.9 0.0 copy-done.1
  0.9 0.0 copy-done
  0.9 0.0 copy-done.2
  0.9 30.0 %deconvolve.1 = f32[64,16,128]{2,1,0:T(8,128)S(1)} custom-call(f32[64,16,128]{2,1,0:T(8,128)} %obs.1, s32[64]{0:T(128)S(1)} %copy-done.2, f32[8,7]{1,0:T(8,128)S(1)} %copy-done, f32[8,7]{1,0:T(8,128)S(1)} %copy-done.1, f32[17]{0:T(128)S(1)} %copy-done.3, s32[4,4,2]{2,1,0:T(4,128)S(1)} %copy.7.stitch), custom_call_target="tpu_custom_call" | custom-call | tf_op jit(solution)/shard_map/deconvolve/pallas_call | solution.py:439
  30.9 0.8 %copy.9 = f32[64,16,128]{2,1,0:T(8,128)} copy(f32[64,16,128]{2,1,0:T(8,128)S(1)} %deconvolve.1) | data formatting | bytes 1048576
Async XLA Ops:
  0.0 0.9 %copy-start.3 = (f32[17]{0:T(128)S(1)}, f32[17]{0:T(128)}, u32[]{:S(2)}) copy-start(f32[17]{0:T(128)} %psf.1) | copy-start | bytes 208
  0.0 0.9 %copy-start.1 = (f32[8,7]{1,0:T(8,128)S(1)}, f32[8,7]{1,0:T(8,128)}, u32[]{:S(2)}) copy-start(f32[8,7]{1,0:T(8,128)} %lat_y.1) | copy-start | bytes 676
  0.0 0.9 %copy-start = (f32[8,7]{1,0:T(8,128)S(1)}, f32[8,7]{1,0:T(8,128)}, u32[]{:S(2)}) copy-start(f32[8,7]{1,0:T(8,128)} %lat_x.1) | copy-start | bytes 676
  0.0 0.9 %copy-start.2 = (s32[64]{0:T(128)S(1)}, s32[64]{0:T(128)}, u32[]{:S(2)}) copy-start(s32[64]{0:T(128)} %zone.1) | copy-start | bytes 772

commit v5 on v4

--- a/solution.py
+++ b/solution.py
@@ -28,7 +28,7 @@
     obs, zone, lat_x, lat_y, psf, stitch, out,
     est1, est2, spr1, spr2, pk, qk, ye1, ye2, ys1, ys2, qe1, qe2, qs1, qs2, ch, lest, rnorm, res,
     ktab, taps, tb, smat, scr, pmain, pnorm, in_sem, out_sem, t_sem,
-    es1, er1, es2, er2, ss1, sr1, ss2, sr2,
+    es, er1, er2, ss, sr1, sr2,
 ):
     sx, sy, gz = lax.axis_index("sx"), lax.axis_index("sy"), lax.axis_index("gz")
     lane = lax.broadcasted_iota(jnp.int32, (8, 128), 1)
@@ -42,7 +42,7 @@
             return slice(g * 8 + off, g * 8 + off + 8)
         return pl.ds(pl.multiple_of(g * 8 + off, 8), 8)
 
-    loads = [pltpu.make_async_copy(obs.at[:, x, :], est1.at[R + x, pl.ds(HZ, NZ)], in_sem.at[x]) for x in range(NX)]
+    loads = [pltpu.make_async_copy(obs.at[:, x, :], est1.at[R + x, pl.ds(HZ, NZ)], in_sem) for x in range(NX)]
     for c in loads:
         c.start()
 
@@ -132,9 +132,14 @@
             ch[0, g * 8 : g * 8 + 8, :] = jnp.where(lane < 110, cd, cu)
             ch[1, g * 8 : g * 8 + 8, :] = cd
 
+    def place_of(dx, dy, dz):
+        if (dx, dy) == (0, 0):
+            return 8 if dz > 0 else 9
+        return [d for d in itertools.product((-1, 0, 1), repeat=2) if d != (0, 0)].index((dx, dy))
+
     def copies(main, strips, packed, corners, cpacked, halo, dirs, send, recv):
         found = {}
-        for i, (dx, dy, dz) in enumerate(dirs):
+        for dx, dy, dz in dirs:
             zs, zd, n = {0: (0, halo, NZ), 1: (NZ - HZ, 0, HZ), -1: (0, halo + NZ, HZ)}[dz]
             if dy == 0:
                 xs, xd, m = {0: (R, R, NX), 1: (NX, 0, R), -1: (R, R + NX, R)}[dx]
@@ -146,9 +151,22 @@
             else:
                 src = cpacked.at[list(CORNERS).index((dx, dy))]
                 dst = corners.at[0 if dy > 0 else 1, 0 if dx > 0 else 1, 1 - dz]
+            k = place_of(dx, dy, dz)
             found[(dx, dy, dz)] = pltpu.make_async_remote_copy(
-                src_ref=src, dst_ref=dst, send_sem=send.at[i], recv_sem=recv.at[i],
+                src_ref=src, dst_ref=dst, send_sem=send.at[k], recv_sem=recv.at[k],
                 device_id=device(dx, dy, dz), device_id_type=MESH)
+            if dz == 0:
+                if dy == 0:
+                    whole = main.at[pl.ds(xd, m)]
+                elif dx == 0:
+                    whole = strips.at[0 if dy > 0 else 1]
+                elif halo:
+                    whole = corners.at[0 if dy > 0 else 1, 0 if dx > 0 else 1]
+                else:
+                    whole = dst
+                found[(dx, dy)] = pltpu.make_async_remote_copy(
+                    src_ref=whole, dst_ref=whole, send_sem=send.at[k], recv_sem=recv.at[k],
+                    device_id=device(dx, dy, 0), device_id_type=MESH)
         return found
 
     X_FACE, Z_FACE, Y_FACE = [(1, 0, 0), (-1, 0, 0)], [(0, 0, 1), (0, 0, -1)], [(0, 1, 0), (0, -1, 0)]
@@ -156,11 +174,14 @@
     YZ = [(0, dy, dz) for dy in (1, -1) for dz in (1, -1)]
     CORN = [(dx, dy, dz) for dx in (1, -1) for dy in (1, -1) for dz in (0, 1, -1)]
     XS = XZ + X_FACE
+    WAITS = X_FACE + [d for d in CORN if d[2] == 0] + Y_FACE + Z_FACE
     SIDES = [(0, dy, dz) for dy in (1, -1) for dz in (1, -1, 0)]
 
     def each(found, sign, what, which):
         for (dx, dy), ds in itertools.groupby([d for d in which if d in found], key=lambda d: d[:2]):
-            def go(ds=tuple(ds)):
+            def go(ds=tuple(ds), dx=dx, dy=dy):
+                if what != "start" and (dx, dy) in found:
+                    ds = [(dx, dy)]
                 for d in ds:
                     getattr(found[d], what)()
             guarded(inside(sign * dx, sign * dy), go)
@@ -282,8 +303,8 @@
 
     nx = 3 - (sx == 0).astype(jnp.int32) - (sx == SX - 1).astype(jnp.int32)
     ny = 3 - (sy == 0).astype(jnp.int32) - (sy == SY - 1).astype(jnp.int32)
-    for c in loads:
-        c.wait()
+    mine = est1.at[pl.ds(R, NX), pl.ds(HZ, NZ)]
+    pltpu.make_async_copy(mine, mine, in_sem).wait()
     pl.semaphore_wait(barrier, nx * ny * 3 - 1)
 
     tcopies = [
@@ -292,10 +313,10 @@
             send_sem=t_sem.at[0, i], recv_sem=t_sem.at[1, i], device_id=device(0, 0, dz), device_id_type=MESH)
         for i, (dz, s, d) in enumerate(((1, NZ, 0), (-1, HZ, HZ + NZ)))
     ]
-    e1 = copies(est1, ye1, pk.at[0], qe1, qk.at[0], HZ, DIRS, es1, er1)
-    s1 = copies(spr1, ys1, pk.at[1], qs1, qk.at[1], 0, SDIRS, ss1, sr1)
-    e2 = copies(est2, ye2, pk.at[2], qe2, qk.at[2], HZ, DIRS, es2, er2)
-    s2 = copies(spr2, ys2, pk.at[3], qs2, qk.at[3], 0, SDIRS, ss2, sr2)
+    e1 = copies(est1, ye1, pk.at[0], qe1, qk.at[0], HZ, DIRS, es, er1)
+    s1 = copies(spr1, ys1, pk.at[1], qs1, qk.at[1], 0, SDIRS, ss, sr1)
+    e2 = copies(est2, ye2, pk.at[2], qe2, qk.at[2], HZ, DIRS, es, er2)
+    s2 = copies(spr2, ys2, pk.at[3], qs2, qk.at[3], 0, SDIRS, ss, sr2)
 
     def packed_groups(k):
         return [pk[k, 8 * g : 8 * g + 8, :] for g in range(NZ // 8)]
@@ -378,12 +399,14 @@
     ):
         if last:
             conv(rows_from(est), False, INNER, 2, 10, 0, 2, 2, keep_lest)
-        each(ecop, -1, "wait_recv", XZ + X_FACE + Z_FACE + CORN + SIDES)
+        each(ecop, -1, "wait_recv", WAITS)
         unpack_corners(qe, HZ)
         halo_strips(*strips_from(ye), False, 0)
         conv(rows_from(est), False, EDGE, 0, EZ // 8, 0, 2, 6, keep_lest)
         strip = [jnp.zeros((8, 128), F32) for _ in range(NZ // 8)]
         strip = depth(((0, 1), (2, 13), (14, 15)), spr, strip)
+        if last:
+            each(s1, 1, "wait_send", WAITS)
         each(scop, 1, "start", X_FACE)
         pack_corners(strip, qk.at[pks])
         each(scop, 1, "start", CORN)
@@ -398,7 +421,7 @@
         if not last:
             halo_strips(*[jnp.concatenate([v] * (NZ // 8), axis=0) for v in wstrips_at], True, HZ)
             conv(lambda x, g: wrows[x], True, tuple(range(NX)), 0, NZ // 8, HZ, 1, 4, keep_norm)
-        each(scop, -1, "wait_recv", X_FACE + CORN + Y_FACE)
+        each(scop, -1, "wait_recv", WAITS)
         unpack_corners(qs, 0)
         halo_strips(*strips_from(ys), True, HZ)
         conv(rows_from(spr), True, EDGE, 0, NZ // 8, HZ, 2, 4, keep_update)
@@ -412,6 +435,7 @@
         else:
             for x in EDGE:
                 est2[R + x, HZ : HZ + NZ, :] = update(x)
+            each(e1, 1, "wait_send", WAITS)
             each(e2, 1, "start", XS)
             pk[2] = pk[0] * (pmain[...] + scr[0:NZ, :]) * pnorm[...]
             pack_corners(packed_groups(2), qk.at[2])
@@ -419,15 +443,14 @@
                 est2[R + x, HZ : HZ + NZ, :] = update(x)
             each(e2, 1, "start", Z_FACE + CORN + SIDES)
 
-    stores = [pltpu.make_async_copy(res.at[x], out.at[:, x, :], out_sem.at[x]) for x in range(NX)]
+    stores = [pltpu.make_async_copy(res.at[x], out.at[:, x, :], out_sem) for x in range(NX)]
     for c in stores:
         c.start()
     for c in tcopies:
         c.wait_send()
-    for found in (e1, s1, e2, s2):
-        each(found, 1, "wait_send", XS + Z_FACE + CORN + SIDES)
-    for c in stores:
-        c.wait()
+    for found in (e2, s2):
+        each(found, 1, "wait_send", WAITS)
+    pltpu.make_async_copy(res, res, out_sem).wait()
 
 
 def body(observed, zone_of_slice, lateral_x, lateral_y, depth_psf, stitch_width):
@@ -435,7 +458,6 @@
     smem = pl.BlockSpec(memory_space=pltpu.SMEM)
     vmem = pl.BlockSpec(memory_space=pltpu.VMEM)
     dma = pltpu.SemaphoreType.DMA
-    ne, ns = len(DIRS), len(SDIRS)
     return pl.pallas_call(
         kernel,
         out_shape=jax.ShapeDtypeStruct(observed.shape, F32),
@@ -454,9 +476,8 @@
             pltpu.VMEM((8, 128), F32), pltpu.VMEM((EZ, 128), F32), pltpu.VMEM((26, EZ, 128), F32),
             pltpu.VMEM((3, 256, 256), BF16), pltpu.VMEM((EZ, 128), F32),
             pltpu.VMEM((NZ, 128), F32), pltpu.VMEM((NZ, 128), F32),
-            dma((NX,)), dma((NX,)), dma((2, 2)),
-            dma((ne,)), dma((ne,)), dma((ne,)), dma((ne,)),
-            dma((ns,)), dma((ns,)), dma((ns,)), dma((ns,)),
+            dma(()), dma(()), dma((2, 2)),
+            dma((10,)), dma((10,)), dma((10,)), dma((8,)), dma((8,)), dma((8,)),
         ],
         compiler_params=pltpu.CompilerParams(collective_id=0, has_side_effects=True, vmem_limit_bytes=54500 * 1024),
         name="deconvolve",

time: 32.3 us -> 31.2 us (0.966)
  Pallas kernels: 30 us -> 28.9 us
    pallas_call x1, Pallas kernels: 30 us -> 28.9 us  [body(): pl.pallas_call(kernel, out_shape=jax.ShapeDtypeStruct(observed.shape, F32...]
where the time goes in v5:
time: 31.2 us; the launch traced here: 30.6 us
  Pallas kernels  28.9 us (93%)
  local copies, waits for them, and re-layouts  1.65 us (5%)
    pallas_call x1, Pallas kernels, body(): pl.pallas_call(kernel, out_shape=jax.ShapeDtypeStruct(observed.shape, F32...  28.9 us
    unnamed x10, local copies, waits for them, and re-layouts  1.65 us

profile of v5, /device:TPU:2, one launch (start us, length us, event | category | flops | bytes accessed | tf_op | source)
XLA Modules:
  0.0 30.6 jit_solution(1278203243429038937)
XLA Ops:
  0.0 0.0 copy-start.3
  0.0 0.0 copy-start.1
  0.0 0.0 copy-start
  0.0 0.0 copy-start.2
  0.0 0.8 %copy.7.stitch = s32[4,4,2]{2,1,0:T(4,128)S(1)} copy(s32[4,4,2]{1,2,0:T(2,128)} %param.11) | data formatting | bytes 256 | tf_op args[5]
  0.9 0.0 copy-done.3
  0.9 0.0 copy-done.1
  0.9 0.0 copy-done
  0.9 0.0 copy-done.2
  0.9 28.9 %deconvolve.1 = f32[64,16,128]{2,1,0:T(8,128)S(1)} custom-call(f32[64,16,128]{2,1,0:T(8,128)} %obs.1, s32[64]{0:T(128)S(1)} %copy-done.2, f32[8,7]{1,0:T(8,128)S(1)} %copy-done, f32[8,7]{1,0:T(8,128)S(1)} %copy-done.1, f32[17]{0:T(128)S(1)} %copy-done.3, s32[4,4,2]{2,1,0:T(4,128)S(1)} %copy.7.stitch), custom_call_target="tpu_custom_call" | custom-call | tf_op jit(solution)/shard_map/deconvolve/pallas_call | solution.py:461
  29.8 0.8 %copy.9 = f32[64,16,128]{2,1,0:T(8,128)} copy(f32[64,16,128]{2,1,0:T(8,128)S(1)} %deconvolve.1) | data formatting | bytes 1048576
Async XLA Ops:
  0.0 0.9 %copy-start.3 = (f32[17]{0:T(128)S(1)}, f32[17]{0:T(128)}, u32[]{:S(2)}) copy-start(f32[17]{0:T(128)} %psf.1) | copy-start | bytes 208
  0.0 0.9 %copy-start.1 = (f32[8,7]{1,0:T(8,128)S(1)}, f32[8,7]{1,0:T(8,128)}, u32[]{:S(2)}) copy-start(f32[8,7]{1,0:T(8,128)} %lat_y.1) | copy-start | bytes 676
  0.0 0.9 %copy-start = (f32[8,7]{1,0:T(8,128)S(1)}, f32[8,7]{1,0:T(8,128)}, u32[]{:S(2)}) copy-start(f32[8,7]{1,0:T(8,128)} %lat_x.1) | copy-start | bytes 676
  0.0 0.9 %copy-start.2 = (s32[64]{0:T(128)S(1)}, s32[64]{0:T(128)}, u32[]{:S(2)}) copy-start(s32[64]{0:T(128)} %zone.1) | copy-start | bytes 772

commit v6 on v5

--- a/solution.py
+++ b/solution.py
@@ -25,7 +25,8 @@
 
 
 def kernel(
-    obs, zone, lat_x, lat_y, psf, stitch, out,
+    obs, zone_in, lat_x_in, lat_y_in, psf_in, stitch_in, out,
+    zone, lat_x, lat_y, psf, stitch, small_sem,
     est1, est2, spr1, spr2, pk, qk, ye1, ye2, ys1, ys2, qe1, qe2, qs1, qs2, ch, lest, rnorm, res,
     ktab, taps, tb, smat, scr, pmain, pnorm, in_sem, out_sem, t_sem,
     es, er1, er2, ss, sr1, sr2,
@@ -43,7 +44,11 @@
         return pl.ds(pl.multiple_of(g * 8 + off, 8), 8)
 
     loads = [pltpu.make_async_copy(obs.at[:, x, :], est1.at[R + x, pl.ds(HZ, NZ)], in_sem) for x in range(NX)]
-    for c in loads:
+    smalls = [
+        pltpu.make_async_copy(a, b, small_sem.at[i])
+        for i, (a, b) in enumerate(((zone_in, zone), (lat_x_in, lat_x), (lat_y_in, lat_y), (psf_in, psf), (stitch_in, stitch)))
+    ]
+    for c in loads + smalls:
         c.start()
 
     def inside(dx, dy):
@@ -255,6 +260,56 @@
         n = ref.shape[1]
         return jnp.where(lane_all[:n] % 6 < R, ref[0], ref[1]), ch[0, 0:n, :], ch[1, 0:n, :]
 
+    def depth_matrix(m, k, forward):
+        off = lax.broadcasted_iota(jnp.int32, (m, k), 1) - lax.broadcasted_iota(jnp.int32, (m, k), 0)
+        h = jnp.zeros((m, k), F32)
+        for j in range(17):
+            h = jnp.where(off == j, psf[16 - j if forward else j], h)
+        h = h / jnp.full((m, k), total, F32)
+        hi = h.astype(BF16)
+        lo = (h - hi.astype(F32)).astype(BF16)
+        return jnp.concatenate([hi, hi, lo], axis=1)
+
+    def split3(v):
+        hi = v.astype(BF16)
+        lo = (v - hi.astype(F32)).astype(BF16)
+        return hi, lo
+
+    nx = 3 - (sx == 0).astype(jnp.int32) - (sx == SX - 1).astype(jnp.int32)
+    ny = 3 - (sy == 0).astype(jnp.int32) - (sy == SY - 1).astype(jnp.int32)
+    for c in smalls:
+        c.wait()
+    mine = est1.at[pl.ds(R, NX), pl.ds(HZ, NZ)]
+    pltpu.make_async_copy(mine, mine, in_sem).wait()
+    pl.semaphore_wait(barrier, nx * ny * 3 - 1)
+
+    tcopies = [
+        pltpu.make_async_remote_copy(
+            src_ref=taps.at[pl.ds(s, HZ), :], dst_ref=taps.at[pl.ds(d, HZ), :],
+            send_sem=t_sem.at[0, i], recv_sem=t_sem.at[1, i], device_id=device(0, 0, dz), device_id_type=MESH)
+        for i, (dz, s, d) in enumerate(((1, NZ, 0), (-1, HZ, HZ + NZ)))
+    ]
+    e1 = copies(est1, ye1, pk.at[0], qe1, qk.at[0], HZ, DIRS, es, er1)
+    s1 = copies(spr1, ys1, pk.at[1], qs1, qk.at[1], 0, SDIRS, ss, sr1)
+    e2 = copies(est2, ye2, pk.at[2], qe2, qk.at[2], HZ, DIRS, es, er2)
+    s2 = copies(spr2, ys2, pk.at[3], qs2, qk.at[3], 0, SDIRS, ss, sr2)
+
+    def packed_groups(k):
+        return [pk[k, 8 * g : 8 * g + 8, :] for g in range(NZ // 8)]
+
+    each(e1, 1, "start", XS + Z_FACE)
+    pack_block(est1, HZ, pk.at[0])
+    pack_corners(packed_groups(0), qk.at[0])
+    each(e1, 1, "start", CORN + SIDES)
+
+    ktab[...] = jnp.zeros((8, 128), F32)
+    ktab[:, 0:7] = lat_x[...]
+    ktab[:, 7:14] = lat_y[...]
+    for z in range(NZ):
+        taps[HZ + z : HZ + z + 1, :] = ktab[pl.ds(zone[z], 1), :]
+    for c in tcopies:
+        c.start()
+
     def band(i, j, k):
         row = stitch[pl.ds(jnp.clip(sx + i, 0, SX - 1), 1), pl.ds(jnp.clip(sy + j, 0, SY - 1), 1), :]
         return jnp.broadcast_to(row[0, :, k : k + 1], (8, 128))
@@ -285,54 +340,6 @@
     total = psf[0]
     for j in range(1, 17):
         total = total + psf[j]
-
-    def depth_matrix(m, k, forward):
-        off = lax.broadcasted_iota(jnp.int32, (m, k), 1) - lax.broadcasted_iota(jnp.int32, (m, k), 0)
-        h = jnp.zeros((m, k), F32)
-        for j in range(17):
-            h = jnp.where(off == j, psf[16 - j if forward else j], h)
-        h = h / jnp.full((m, k), total, F32)
-        hi = h.astype(BF16)
-        lo = (h - hi.astype(F32)).astype(BF16)
-        return jnp.concatenate([hi, hi, lo], axis=1)
-
-    def split3(v):
-        hi = v.astype(BF16)
-        lo = (v - hi.astype(F32)).astype(BF16)
-        return hi, lo
-
-    nx = 3 - (sx == 0).astype(jnp.int32) - (sx == SX - 1).astype(jnp.int32)
-    ny = 3 - (sy == 0).astype(jnp.int32) - (sy == SY - 1).astype(jnp.int32)
-    mine = est1.at[pl.ds(R, NX), pl.ds(HZ, NZ)]
-    pltpu.make_async_copy(mine, mine, in_sem).wait()
-    pl.semaphore_wait(barrier, nx * ny * 3 - 1)
-
-    tcopies = [
-        pltpu.make_async_remote_copy(
-            src_ref=taps.at[pl.ds(s, HZ), :], dst_ref=taps.at[pl.ds(d, HZ), :],
-            send_sem=t_sem.at[0, i], recv_sem=t_sem.at[1, i], device_id=device(0, 0, dz), device_id_type=MESH)
-        for i, (dz, s, d) in enumerate(((1, NZ, 0), (-1, HZ, HZ + NZ)))
-    ]
-    e1 = copies(est1, ye1, pk.at[0], qe1, qk.at[0], HZ, DIRS, es, er1)
-    s1 = copies(spr1, ys1, pk.at[1], qs1, qk.at[1], 0, SDIRS, ss, sr1)
-    e2 = copies(est2, ye2, pk.at[2], qe2, qk.at[2], HZ, DIRS, es, er2)
-    s2 = copies(spr2, ys2, pk.at[3], qs2, qk.at[3], 0, SDIRS, ss, sr2)
-
-    def packed_groups(k):
-        return [pk[k, 8 * g : 8 * g + 8, :] for g in range(NZ // 8)]
-
-    each(e1, 1, "start", XS + Z_FACE)
-    pack_block(est1, HZ, pk.at[0])
-    pack_corners(packed_groups(0), qk.at[0])
-    each(e1, 1, "start", CORN + SIDES)
-
-    ktab[...] = jnp.zeros((8, 128), F32)
-    ktab[:, 0:7] = lat_x[...]
-    ktab[:, 7:14] = lat_y[...]
-    for z in range(NZ):
-        taps[HZ + z : HZ + z + 1, :] = ktab[pl.ds(zone[z], 1), :]
-    for c in tcopies:
-        c.start()
 
     row = lax.broadcasted_iota(jnp.int32, (256, 128), 0) % 128
     col = lax.broadcasted_iota(jnp.int32, (256, 128), 1)
@@ -455,15 +462,15 @@
 
 def body(observed, zone_of_slice, lateral_x, lateral_y, depth_psf, stitch_width):
     hbm = pl.BlockSpec(memory_space=pltpu.HBM)
-    smem = pl.BlockSpec(memory_space=pltpu.SMEM)
-    vmem = pl.BlockSpec(memory_space=pltpu.VMEM)
     dma = pltpu.SemaphoreType.DMA
     return pl.pallas_call(
         kernel,
         out_shape=jax.ShapeDtypeStruct(observed.shape, F32),
-        in_specs=[hbm, smem, vmem, vmem, smem, vmem],
+        in_specs=[hbm] * 6,
         out_specs=hbm,
         scratch_shapes=[
+            pltpu.SMEM((NZ,), jnp.int32), pltpu.VMEM((8, 7), F32), pltpu.VMEM((8, 7), F32),
+            pltpu.SMEM((17,), F32), pltpu.VMEM((SX, SY, 2), jnp.int32), dma((5,)),
             pltpu.VMEM((EX, EZ, NY), F32), pltpu.VMEM((EX, EZ, NY), F32),
             pltpu.VMEM((EX, NZ, NY), F32), pltpu.VMEM((EX, NZ, NY), F32),
             pltpu.VMEM((4, NZ, 128), F32), pltpu.VMEM((4, 4, 8, 128), F32),

time: 31.2 us -> 30.8 us (0.987)
  Pallas kernels: 28.9 us -> 28.5 us
    pallas_call x1, Pallas kernels: 28.9 us -> 28.5 us  [body(): pl.pallas_call(kernel, out_shape=jax.ShapeDtypeStruct(observed.shape, F32...]
where the time goes in v6:
time: 30.8 us; the launch traced here: 30.1 us
  Pallas kernels  28.5 us (93%)
  local copies, waits for them, and re-layouts  1.65 us (5%)
    pallas_call x1, Pallas kernels, body(): pl.pallas_call(kernel, out_shape=jax.ShapeDtypeStruct(observed.shape, F32...  28.5 us
    unnamed x10, local copies, waits for them, and re-layouts  1.65 us

profile of v6, /device:TPU:2, one launch (start us, length us, event | category | flops | bytes accessed | tf_op | source)
XLA Modules:
  0.0 30.1 jit_solution(9765111569260417000)
XLA Ops:
  0.0 0.0 copy-start.3
  0.0 0.0 copy-start.1
  0.0 0.0 copy-start
  0.0 0.0 copy-start.2
  0.0 0.8 %copy.7.stitch_in = s32[4,4,2]{2,1,0:T(4,128)S(1)} copy(s32[4,4,2]{1,2,0:T(2,128)} %param.11) | data formatting | bytes 256 | tf_op args[5]
  0.9 0.0 copy-done.3
  0.9 0.0 copy-done.1
  0.9 0.0 copy-done
  0.9 0.0 copy-done.2
  0.9 28.5 %deconvolve.1 = f32[64,16,128]{2,1,0:T(8,128)S(1)} custom-call(f32[64,16,128]{2,1,0:T(8,128)} %obs.1, s32[64]{0:T(128)S(1)} %copy-done.2, f32[8,7]{1,0:T(8,128)S(1)} %copy-done, f32[8,7]{1,0:T(8,128)S(1)} %copy-done.1, f32[17]{0:T(128)S(1)} %copy-done.3, s32[4,4,2]{2,1,0:T(4,128)S(1)} %copy.7.stitch_in), custom_call_target="tpu_custom_call" | custom-call | tf_op jit(solution)/shard_map/deconvolve/pallas_call | solution.py:466
  29.3 0.8 %copy.9 = f32[64,16,128]{2,1,0:T(8,128)} copy(f32[64,16,128]{2,1,0:T(8,128)S(1)} %deconvolve.1) | data formatting | bytes 1048576
Async XLA Ops:
  0.0 0.9 %copy-start.3 = (f32[17]{0:T(128)S(1)}, f32[17]{0:T(128)}, u32[]{:S(2)}) copy-start(f32[17]{0:T(128)} %psf_in.1) | copy-start | bytes 208
  0.0 0.9 %copy-start.1 = (f32[8,7]{1,0:T(8,128)S(1)}, f32[8,7]{1,0:T(8,128)}, u32[]{:S(2)}) copy-start(f32[8,7]{1,0:T(8,128)} %lat_y_in.1) | copy-start | bytes 676
  0.0 0.9 %copy-start = (f32[8,7]{1,0:T(8,128)S(1)}, f32[8,7]{1,0:T(8,128)}, u32[]{:S(2)}) copy-start(f32[8,7]{1,0:T(8,128)} %lat_x_in.1) | copy-start | bytes 676
  0.0 0.9 %copy-start.2 = (s32[64]{0:T(128)S(1)}, s32[64]{0:T(128)}, u32[]{:S(2)}) copy-start(s32[64]{0:T(128)} %zone_in.1) | copy-start | bytes 772

commit v7 on v6

--- a/solution.py
+++ b/solution.py
@@ -414,9 +414,8 @@
         strip = depth(((0, 1), (2, 13), (14, 15)), spr, strip)
         if last:
             each(s1, 1, "wait_send", WAITS)
-        each(scop, 1, "start", X_FACE)
         pack_corners(strip, qk.at[pks])
-        each(scop, 1, "start", CORN)
+        each(scop, 1, "start", CORN + X_FACE)
         conv(rows_from(est), False, INNER, 0, 2, 0, 2, 1, keep_lest)
         conv(rows_from(est), False, INNER, 10, 12, 0, 2, 1, keep_lest)
         strip = depth(((3, 4), (5, 6), (7, 8), (9, 10), (11, 12)), spr, strip)
@@ -448,7 +447,7 @@
             pack_corners(packed_groups(2), qk.at[2])
             for x in INNER:
                 est2[R + x, HZ : HZ + NZ, :] = update(x)
-            each(e2, 1, "start", Z_FACE + CORN + SIDES)
+            each(e2, 1, "start", CORN + SIDES + Z_FACE)
 
     stores = [pltpu.make_async_copy(res.at[x], out.at[:, x, :], out_sem) for x in range(NX)]
     for c in stores:

time: 30.8 us -> 30.8 us (level)
  no operation moved by 1% of the time
where the time goes in v7:
time: 30.8 us; the launch traced here: 30.3 us
  Pallas kernels  28.7 us (93%)
  local copies, waits for them, and re-layouts  1.65 us (5%)
    pallas_call x1, Pallas kernels, body(): pl.pallas_call(kernel, out_shape=jax.ShapeDtypeStruct(observed.shape, F32...  28.7 us
    unnamed x10, local copies, waits for them, and re-layouts  1.65 us

profile of v7, /device:TPU:2, one launch (start us, length us, event | category | flops | bytes accessed | tf_op | source)
XLA Modules:
  0.0 30.3 jit_solution(378494355386535285)
XLA Ops:
  0.0 0.0 copy-start.3
  0.0 0.0 copy-start.1
  0.0 0.0 copy-start
  0.0 0.0 copy-start.2
  0.0 0.8 %copy.7.stitch_in = s32[4,4,2]{2,1,0:T(4,128)S(1)} copy(s32[4,4,2]{1,2,0:T(2,128)} %param.11) | data formatting | bytes 256 | tf_op args[5]
  0.9 0.0 copy-done.3
  0.9 0.0 copy-done.1
  0.9 0.0 copy-done
  0.9 0.0 copy-done.2
  0.9 28.7 %deconvolve.1 = f32[64,16,128]{2,1,0:T(8,128)S(1)} custom-call(f32[64,16,128]{2,1,0:T(8,128)} %obs.1, s32[64]{0:T(128)S(1)} %copy-done.2, f32[8,7]{1,0:T(8,128)S(1)} %copy-done, f32[8,7]{1,0:T(8,128)S(1)} %copy-done.1, f32[17]{0:T(128)S(1)} %copy-done.3, s32[4,4,2]{2,1,0:T(4,128)S(1)} %copy.7.stitch_in), custom_call_target="tpu_custom_call" | custom-call | tf_op jit(solution)/shard_map/deconvolve/pallas_call | solution.py:465
  29.5 0.8 %copy.9 = f32[64,16,128]{2,1,0:T(8,128)} copy(f32[64,16,128]{2,1,0:T(8,128)S(1)} %deconvolve.1) | data formatting | bytes 1048576
Async XLA Ops:
  0.0 0.9 %copy-start.3 = (f32[17]{0:T(128)S(1)}, f32[17]{0:T(128)}, u32[]{:S(2)}) copy-start(f32[17]{0:T(128)} %psf_in.1) | copy-start | bytes 208
  0.0 0.9 %copy-start.1 = (f32[8,7]{1,0:T(8,128)S(1)}, f32[8,7]{1,0:T(8,128)}, u32[]{:S(2)}) copy-start(f32[8,7]{1,0:T(8,128)} %lat_y_in.1) | copy-start | bytes 676
  0.0 0.9 %copy-start = (f32[8,7]{1,0:T(8,128)S(1)}, f32[8,7]{1,0:T(8,128)}, u32[]{:S(2)}) copy-start(f32[8,7]{1,0:T(8,128)} %lat_x_in.1) | copy-start | bytes 676
  0.0 0.9 %copy-start.2 = (s32[64]{0:T(128)S(1)}, s32[64]{0:T(128)}, u32[]{:S(2)}) copy-start(s32[64]{0:T(128)} %zone_in.1) | copy-start | bytes 772
